TPU v7x, 128 devices: a whole 4x4x4 slice. The times are simulated.
128 devices in a mesh: group: 2 (over z_lo), seq: 16 (over x, z_hi, core), dp: 4 (over y).
Axes of the slice: x: 4, y: 4, z: 4 (z_hi: 2, z_lo: 2; z = z_hi * 2 + z_lo), core: 2. Of those that a mesh axis runs over, the one named last changes fastest.
Arguments:
- latent_tokens: bfloat16 [8, 4096, 3072], P(('group', 'dp'), 'seq'), may hold values from -6 to 6
- modulation: float32 [8, 2, 3072], P(('group', 'dp')), may hold values from -3 to 3, as said below
- w_qkv: bfloat16 [3, 3072, 2048], P(None, None, 'seq'), may hold values from -0.108253175 to 0.108253175, as said below
- w_out: bfloat16 [2048, 64], replicated, may hold values from -0.125 to 0.125
- noisy_latents: bfloat16 [8, 16, 4, 32, 128], P(('group', 'dp'), None, None, 'seq'), may hold values from -6 to 6
- queue: int32 [8], replicated, may hold values from 0 to 7, each once
- frame_counts: int32 [8], replicated, may hold values from 1 to 4, 24 in all
- conv_w: bfloat16 [512, 432], replicated, may hold values from -0.3125 to 0.3125
- conv_b: float32 [512], replicated, may hold values from -1 to 1
Outputs:
- attended: bfloat16 [8, 4096, 2048], P(('group', 'dp'), 'seq')
- decoded: bfloat16 [8, 512, 4, 32, 128], P(('group', 'dp'), None, None, 'seq')
Inputs may be any that keep to these rules, and one draw needn't show every extreme that they name: `queue`: each request appears once. `frame_counts`: some request has all 4 frames. `modulation`: row 0 holds the shift, row 1 the scale. `w_qkv`: query, key and value blocks in that order.
All inputs are finite; a program needn't handle non-finite values.
Results may differ from a plain program's by a relative error of at most 0.012.
Values may be sent and summed in bfloat16 or wider, within the bound.
No kernel may reach another device: no remote copies, remote signals or barrier semaphores. Data moves between devices by JAX's collectives and lax.ppermute only.
A program may use at most 192 MiB of HBM per device.

v0:
```python
import jax
import jax.numpy as jnp
from jax import lax
from jax.sharding import PartitionSpec as P

HEAD_DIM = 128


def padded_2(array, sides, width):
    for axis, dim in sides:
        size, length = (lax.axis_size(axis), array.shape[dim])
        up = [(i, (i + 1) % size) for i in range(size - 1)]
        down = [(j, i) for i, j in up]
        last = lax.slice_in_dim(array, length - width, length, axis=dim)
        initial = lax.slice_in_dim(array, 0, width, axis=dim)
        before = lax.ppermute(last, axis, up)
        after = lax.ppermute(initial, axis, down)
        array = jnp.concatenate([before, array, after], axis=dim)
    return array


def local_attention(triple):
    query = triple[0, :, 0:HEAD_DIM]
    keys = triple[1, :, 0:HEAD_DIM]
    vals = triple[2, :, 0:HEAD_DIM]
    scores = jnp.dot(query, keys.T, preferred_element_type=jnp.float32) / jnp.sqrt(
        jnp.float32(HEAD_DIM)
    )
    probs = jax.nn.softmax(scores, axis=-1).astype(jnp.bfloat16)
    outputs = jnp.dot(probs, vals, preferred_element_type=jnp.float32).astype(jnp.bfloat16)
    return outputs


def update_rows(attended, noisy, w_out):
    values = attended.astype(jnp.float32)
    final_normed = (
        values * lax.rsqrt(jnp.mean(values * values, axis=-1, keepdims=True) + 1e-06)
    ).astype(jnp.bfloat16)
    predicted = jnp.dot(final_normed, w_out, preferred_element_type=jnp.float32)
    channels = noisy.shape[0]
    frames = noisy.shape[1]
    rows = noisy.shape[2]
    columns = noisy.shape[3]
    grid = predicted.reshape(rows // 2, frames, columns // 2, channels, 2, 2)
    grid = grid.transpose(3, 1, 0, 4, 2, 5).reshape(channels, frames, rows, columns)
    return (noisy.astype(jnp.float32) + grid).astype(jnp.bfloat16)


def causal_features(padded, limit, conv_w, conv_b):
    frames = padded.shape[1]
    rows = padded.shape[2] - 2
    columns = padded.shape[3]
    first = padded[:, :1]
    padded = jnp.concatenate([first, first, padded], axis=1)
    padded = jnp.pad(padded, ((0, 0), (0, 0), (0, 0), (1, 1)))
    slices = []
    for step_t in range(3):
        for step_h in range(3):
            for step_w in range(3):
                slices.append(
                    padded[
                        :,
                        step_t : step_t + frames,
                        step_h : step_h + rows,
                        step_w : step_w + columns,
                    ]
                )
    stacked = jnp.stack(slices, 0).reshape(27 * padded.shape[0], frames * rows * columns)
    features = jnp.dot(conv_w, stacked, preferred_element_type=jnp.float32) + conv_b[:, None]
    features = features.reshape(conv_w.shape[0], frames, rows, columns)
    frame_ids = jnp.arange(frames, dtype=jnp.int32)
    keep = (frame_ids < limit).astype(jnp.float32)
    return (features * keep[None, :, None, None]).astype(jnp.bfloat16)


def on_device(
    latent_tokens, modulation, w_qkv, w_out, noisy_latents, queue, frame_counts, conv_w, conv_b
):
    values = latent_tokens[0].astype(jnp.float32)
    shift_scale = modulation[0]
    scaled = values * lax.rsqrt(jnp.mean(values * values, axis=-1, keepdims=True) + 1e-06)
    normed = (scaled * (1.0 + shift_scale[1]) + shift_scale[0]).astype(jnp.bfloat16)
    projected = jnp.einsum(
        "td,cdh->cth",
        normed,
        lax.all_gather(w_qkv, "seq", axis=2, tiled=True),
        preferred_element_type=jnp.float32,
    ).astype(jnp.bfloat16)
    triple = lax.all_to_all(projected, "seq", split_axis=2, concat_axis=1, tiled=True)
    head_outputs = local_attention(triple)
    attended = lax.all_to_all(head_outputs, "seq", split_axis=0, concat_axis=1, tiled=True)
    new_latent = update_rows(attended, noisy_latents[0], w_out)[None]
    slot_index = lax.axis_index(("group", "dp"))
    source = lax.dynamic_index_in_dim(queue, slot_index, 0, keepdims=False)
    limit = lax.dynamic_index_in_dim(frame_counts, source, 0, keepdims=False)
    everyone = lax.all_gather(new_latent, ("group", "dp"), axis=0, tiled=True)
    chosen = lax.dynamic_index_in_dim(everyone, source, 0, keepdims=False)
    padded = padded_2(chosen, (("seq", 2),), 1)
    decoded = causal_features(padded, limit, conv_w, conv_b)
    return (attended[None], decoded[None])


def solution(mesh):
    return jax.shard_map(
        on_device,
        mesh=mesh,
        in_specs=(
            P(("group", "dp"), "seq", None),
            P(("group", "dp"), None, None),
            P(None, None, "seq"),
            P(),
            P(("group", "dp"), None, None, "seq", None),
            P(),
            P(),
            P(),
            P(),
        ),
        out_specs=(P(("group", "dp"), "seq", None), P(("group", "dp"), None, None, "seq", None)),
        check_vma=False,
    )
```

profile of v0, /device:TPU:1, one launch (start us, length us, event | category | flops | bytes accessed | tf_op | source)
XLA Modules:
  0.0 481.9 jit_solution(15707288944313909320)
XLA Ops:
  7.9 0.7 copy-done.1
  9.1 237.0 %all-gather.2.cloned.1.call-done = bf16[3,3072,2048]{2,1,0:T(8,128)(2,1)} async-done(((bf16[3,3072,128]{2,1,0:T(8,128)(2,1)}), bf16[3,3072,2048]{2,1,0:T(8,128)(2,1)}) %all-gather.2.cloned.1.call-update) | async-done | bytes 37748752 | tf_op jit(solution)/shard_map/all_gather | solution.py:86
  246.1 18.3 %fusion.7 = bf16[3,256,2048]{2,1,0:T(8,128)(2,1)} fusion(bf16[3,3072,2048]{2,1,0:T(8,128)(2,1)} %all-gather.2.cloned.1.call-done, bf16[1,256,3072]{2,1,0:T(8,128)(2,1)S(1)} %copy-done.1, f32[3072]{0:T(1024)S(1)} %bitcast.162, f32[3072]{0:T(1024)S(1)} %bitcast.161, f32[256]{0:T(256)S(1)} %add_rsqrt_fusion.1), kind=kOutput, calls=%fused_computation.13 | convolution fusion | flops 9669181440 | bytes 42492928 | tf_op jit(solution)/shard_map/td,cdh->cth/dot_general | solution.py:83
  264.4 7.1 %copy.52 = bf16[3,256,2048]{1,0,2:T(4,128)(2,1)} copy(bf16[3,256,2048]{2,1,0:T(8,128)(2,1)} %fusion.7) | data formatting | bytes 6291456 | tf_op jit(solution)/shard_map/convert_element_type | solution.py:88
  271.5 54.3 %all_to_all.31 = bf16[3,256,2048]{1,0,2:T(4,128)(2,1)S(1)} all-to-all(bf16[3,256,2048]{1,0,2:T(4,128)(2,1)} %copy.52), channel_id=1, replica_groups=mesh['group'=2,'seq'=16,'dp'=4] {'seq'}, dimensions={2} | all-to-all | bytes 6291456 | tf_op jit(solution)/shard_map/all_to_all | solution.py:89
  326.3 1.2 fusion.40
  327.5 1.3 copy.56
  329.4 1.6 copy.55
  331.1 24.0 %multiply_reduce_fusion = (f32[4096]{0:T(1024)S(1)}, f32[4096,4096]{0,1:T(8,128)}) fusion(bf16[4096,128]{1,0:T(8,128)(2,1)S(1)} %bitcast.155, bf16[4096,128]{1,0:T(8,128)(2,1)S(1)} %bitcast.156), kind=kOutput, calls=%fused_computation.2 | convolution fusion | flops 4328517632 | bytes 69222400 | tf_op jit(solution)/shard_map/dot_general | solution.py:26
  355.1 21.5 %fusion = f32[4096]{0:T(1024)S(1)} fusion(f32[4096,4096]{0,1:T(8,128)} %get-tuple-element.10, f32[4096]{0:T(1024)S(1)} %get-tuple-element.9), kind=kLoop, calls=%fused_computation.3 | loop fusion | flops 50327552 | bytes 67141632 | tf_op jit(solution)/shard_map/reduce_sum | solution.py:29
  376.6 24.9 %fusion.2 = bf16[4096,128]{1,0:T(8,128)(2,1)} fusion(bf16[4096,128]{1,0:T(8,128)(2,1)S(1)} %bitcast.159, f32[4096,4096]{0,1:T(8,128)} %get-tuple-element.10, f32[4096]{0:T(1024)S(1)} %fusion, f32[4096]{0:T(1024)S(1)} %get-tuple-element.9), kind=kOutput, calls=%fused_computation.5 | convolution fusion | flops 4362600448 | bytes 69238784 | tf_op jit(solution)/shard_map/dot_general | solution.py:30
  401.5 4.8 all-to-all-start.1
  409.6 14.0 %all-to-all-done.1 = bf16[16,256,128]{2,1,0:T(8,128)(2,1)S(1)} async-done(((bf16[16,256,128]{2,1,0:T(8,128)(2,1)}), bf16[16,256,128]{2,1,0:T(8,128)(2,1)S(1)}, u32[]{:S(2)}, u32[]{:S(2)}) %all-to-all-start.1) | async-done | bytes 1048608 | tf_op jit(solution)/shard_map/all_to_all | solution.py:91
  424.9 1.3 reshape.104
  426.2 1.8 convolution_bitcast_fusion
  428.5 22.0 %all_gather.7 = bf16[8,16,4,2,128]{4,1,3,2,0:T(8,128)(2,1)S(1)} all-gather(bf16[1,16,4,2,128]{4,1,3,2,0:T(8,128)(2,1)S(1)} %add_convert_fusion), channel_id=1, replica_groups=mesh['group'=2,'seq'=16,'dp'=4] {'group','dp'}, dimensions={0}, use_global_device_ids=true | all-gather | bytes 294912 | tf_op jit(solution)/shard_map/all_gather | solution.py:96
  450.5 9.1 %collective-permute-start.1 = (bf16[16,4,1,128]{3,0,2,1:T(8,128)(2,1)S(1)}, bf16[16,4,1,128]{3,0,2,1:T(8,128)(2,1)S(1)}, u32[]{:S(2)}, u32[]{:S(2)}) collective-permute-start(bf16[16,4,1,128]{3,0,2,1:T(8,128)(2,1)S(1)} %get-tuple-element.6), channel_id=1, source_target_pairs={{4,0},{8,4},{12,8},{16,12},{20,16},{24,20},{28,24},{32,28},{36,32}... | collective-permute-start | bytes 49160 | tf_op jit(solution)/shard_map/ppermute | solution.py:17
  459.7 2.3 collective-permute-start
  462.7 0.7 copy.57
  463.3 1.3 broadcast_in_dim.2
  466.5 0.9 copy.63
  468.1 2.1 convolution_add_fusion
  470.2 3.2 copy.64
  473.3 1.8 multiply_convert_fusion
  (70 shorter events, 8.4 us)
Async XLA Ops:
  7.2 460.9 %copy-start = (bf16[512,432]{0,1:T(8,128)(2,1)S(1)}, bf16[512,432]{0,1:T(8,128)(2,1)}, u32[]{:S(2)}) copy-start(bf16[512,432]{0,1:T(8,128)(2,1)} %param.16) | copy-start | bytes 1327108
  7.2 1.5 copy-start.1
  7.2 1.9 copy-start.5
  7.2 238.9 %all-gather.2.cloned.1.call-start = ((), (), s32[]{:S(2)}) async-start(), calls=%async_computation.2 | async-start | bytes 40108032 | tf_op jit(solution)/shard_map/all_gather | solution.py:86
  355.1 21.5 %copy-start.2 = (bf16[1,16,256,128]{3,2,1,0:T(8,128)(2,1)S(1)}, bf16[1,16,256,128]{3,2,1,0:T(8,128)(2,1)}, u32[]{:S(2)}) copy-start(bf16[1,16,256,128]{3,2,1,0:T(8,128)(2,1)} %copy.56) | copy-start | bytes 3145732
  376.6 29.7 %copy-start.7 = (s32[8]{0:T(128)S(1)}, s32[8]{0:T(128)}, u32[]{:S(2)}) copy-start(s32[8]{0:T(128)} %param.14) | copy-start | bytes 100
  376.6 31.6 %copy-start.3 = (bf16[2048,64]{0,1:T(8,128)(2,1)S(1)}, bf16[2048,64]{0,1:T(8,128)(2,1)}, u32[]{:S(2)}) copy-start(bf16[2048,64]{0,1:T(8,128)(2,1)} %param.12) | copy-start | bytes 786436
  376.6 32.4 %copy-start.8 = (s32[8]{0:T(128)S(1)}, s32[8]{0:T(128)}, u32[]{:S(2)}) copy-start(s32[8]{0:T(128)} %param.15) | copy-start | bytes 100
  401.5 22.1 %all-to-all-start.1 = ((bf16[16,256,128]{2,1,0:T(8,128)(2,1)}), bf16[16,256,128]{2,1,0:T(8,128)(2,1)S(1)}, u32[]{:S(2)}, u32[]{:S(2)}) async-start(bf16[16,256,128]{2,1,0:T(8,128)(2,1)} %bitcast.12), calls=%async_computation.1 | async-start | bytes 2097152 | tf_op jit(solution)/shard_map/all_to_all | solution.py:91
  424.2 4.3 copy-start.4
  450.5 14.1 %collective-permute-start.1 = (bf16[16,4,1,128]{3,0,2,1:T(8,128)(2,1)S(1)}, bf16[16,4,1,128]{3,0,2,1:T(8,128)(2,1)S(1)}, u32[]{:S(2)}, u32[]{:S(2)}) collective-permute-start(bf16[16,4,1,128]{3,0,2,1:T(8,128)(2,1)S(1)} %get-tuple-element.6), channel_id=1, source_target_pairs={{4,0},{8,4},{12,8},{16,12},{20,16},{24,20},{28,24},{32,28},{36,32}... | collective-permute-start | bytes 49160 | tf_op jit(solution)/shard_map/ppermute | solution.py:17
  459.7 4.9 %collective-permute-start = (bf16[16,4,1,128]{3,0,2,1:T(8,128)(2,1)S(1)}, bf16[16,4,1,128]{3,0,2,1:T(8,128)(2,1)S(1)}, u32[]{:S(2)}, u32[]{:S(2)}) collective-permute-start(bf16[16,4,1,128]{3,0,2,1:T(8,128)(2,1)S(1)} %get-tuple-element.5), channel_id=1, source_target_pairs={{0,4},{4,8},{8,12},{12,16},{16,20},{20,24},{24,28},{28,32},{32,36}... | collective-permute-start | bytes 49160 | tf_op jit(solution)/shard_map/ppermute | solution.py:16
  464.9 3.1 copy-start.6
Sparse Core Ops, SparseCore 0:
  10.3 235.7 all-gather.1
where the time goes:
time: 483 us; the launch traced here: 482 us
  waiting for transfers between devices  252 us (52%)
  blocking collectives  76.3 us (16%)
  matrix products  71.1 us (15%)
  local copies, waits for them, and re-layouts  25.2 us (5%)
  other arithmetic  25 us (5%)
  starting transfers between devices  16.3 us (3%)
  between operations  16.3 us (3%)
    all_gather x1, waiting for transfers between devices, on_device(): lax.all_gather(w_qkv, 'seq', axis=2, tiled=True)  237 us
    all_to_all x1, blocking collectives, on_device(): lax.all_to_all(projected, 'seq', split_axis=2, concat_axis=1, tiled=True)  54.3 us
    dot_general x1, matrix products, local_attention(): jnp.dot(probs, vals, preferred_element_type=jnp.float32)  24.9 us
    dot_general x1, matrix products, local_attention(): jnp.dot(query, keys.T, preferred_element_type=jnp.float32)  24 us
    all_gather x1, blocking collectives, on_device(): everyone = lax.all_gather(new_latent, ('group', 'dp'), axis=0, tiled=True)  22 us
    reduce_sum x1, other arithmetic, local_attention(): probs = jax.nn.softmax(scores, axis=-1).astype(jnp.bfloat16)  21.5 us
    dot_general x1, matrix products, on_device(): jnp.einsum('td,cdh->cth', normed, lax.all_gather(w_qkv, 'seq', axis=2, ti...  18.3 us
    all_to_all x1, waiting for transfers between devices, on_device(): lax.all_to_all(head_outputs, 'seq', split_axis=0, concat_axis=1, tiled=True)  14 us
  transfers between devices with their start and end apart: 4, of which 2 were waited for; matrix products, arithmetic and copies ran while one was open for 1% of the time, Pallas kernels for 0%

commit v1 on v0

--- a/solution.py
+++ b/solution.py
@@ -1,9 +1,154 @@
+import functools
+import math
+
 import jax
 import jax.numpy as jnp
 from jax import lax
+from jax.experimental import pallas as pl
+from jax.experimental.pallas import tpu as pltpu
 from jax.sharding import PartitionSpec as P
 
 HEAD_DIM = 128
+EVERY = ("group", "seq", "dp")
+XS, ZS, YS = (4, 4, 4)
+VMEM_BYTES = 48 << 20
+QUERY_SCALE = math.log2(math.e) / math.sqrt(HEAD_DIM)
+NT = (((1,), (1,)), ((), ()))
+
+
+def linear(x, y, z, core):
+    return ((z % 2) * 16 + (x * 2 + z // 2) * 2 + core) * YS + y
+
+
+def moved(array, move):
+    perm = []
+    for x in range(XS):
+        for y in range(YS):
+            for z in range(ZS):
+                for core in range(2):
+                    to = move(x, y, z, core)
+                    there = linear(to[0] % XS, to[1] % YS, to[2] % ZS, to[3])
+                    perm.append((linear(x, y, z, core), there))
+    return lax.ppermute(array, EVERY, perm)
+
+
+def right(x, y, z, core):
+    return (x + 1, y, z, core)
+
+
+def left(x, y, z, core):
+    return (x - 1, y, z, core)
+
+
+def other_core(x, y, z, core):
+    return (x, y, z, 1 - core)
+
+
+def opposite_z(x, y, z, core):
+    return (x, y, z + 2, core)
+
+
+def mirrored_z(x, y, z, core):
+    return (x, y, 3 - z, core)
+
+
+def project_kernel(n_tokens, part_ref, *refs):
+    tokens = refs[:n_tokens]
+    w_ref = refs[n_tokens]
+    w_parts = refs[n_tokens + 1 : n_tokens + 5]
+    own_ref, away_ref = refs[n_tokens + 5 :]
+    total = None
+    for k in range(4):
+        depth = w_parts[k].shape[1]
+        at = pl.multiple_of(part_ref[k] * depth, depth)
+        rows = jnp.concatenate([t[:, pl.ds(at, depth)] for t in tokens], axis=0)
+        columns = jnp.concatenate([w_ref[0, pl.ds(at, depth), :], w_parts[k][0]], axis=1)
+        term = jnp.dot(rows, columns, preferred_element_type=jnp.float32)
+        total = term if total is None else total + term
+    scale = jnp.where(pl.program_id(0) == 0, jnp.float32(QUERY_SCALE), jnp.float32(1.0))
+    total = (total * scale).astype(jnp.bfloat16)
+    own_ref[0] = total[:, :HEAD_DIM]
+    away_ref[0] = total[:, HEAD_DIM:]
+
+
+def project(parts, tokens, w_qkv, w_parts):
+    rows = sum(t.shape[0] for t in tokens)
+    depth = w_qkv.shape[1]
+    whole = pl.BlockSpec(memory_space=pltpu.VMEM)
+    out = jax.ShapeDtypeStruct((3, rows, HEAD_DIM), jnp.bfloat16)
+    return pl.pallas_call(
+        functools.partial(project_kernel, len(tokens)),
+        grid_spec=pltpu.PrefetchScalarGridSpec(
+            num_scalar_prefetch=1,
+            grid=(3,),
+            in_specs=[whole] * len(tokens)
+            + [pl.BlockSpec((1, depth, HEAD_DIM), lambda c, s: (c, 0, 0))]
+            + [pl.BlockSpec((1, depth // 4, HEAD_DIM), lambda c, s: (c, 0, 0))] * 4,
+            out_specs=[pl.BlockSpec((1, rows, HEAD_DIM), lambda c, s: (c, 0, 0))] * 2,
+        ),
+        out_shape=(out, out),
+        compiler_params=pltpu.CompilerParams(vmem_limit_bytes=VMEM_BYTES),
+        cost_estimate=pl.CostEstimate(
+            flops=rows * depth * 6 * HEAD_DIM * 2,
+            bytes_accessed=rows * depth * 2 + depth * 6 * HEAD_DIM * 2,
+            transcendentals=0,
+        ),
+    )(parts, *tokens, w_qkv, *w_parts)
+
+
+def attention_kernel(n_blocks, chunk, place_ref, *refs):
+    blocks = refs[:n_blocks]
+    out_ref, q_all, k_all, v_all = refs[n_blocks:]
+
+    @pl.when(pl.program_id(0) == 0)
+    def _():
+        rows = blocks[0].shape[1]
+        half = rows // 2
+        for i, block in enumerate(blocks):
+            k_all[i * rows : (i + 1) * rows, :] = block[1]
+            v_all[i * rows : (i + 1) * rows, :] = block[2]
+            for j in range(2):
+                at = pl.multiple_of(place_ref[2 * i + j] * half, half)
+                q_all[pl.ds(at, half), :] = block[0, j * half : (j + 1) * half, :]
+
+    rows = out_ref.shape[0]
+    q = q_all[pl.ds(pl.multiple_of(pl.program_id(0) * rows, rows), rows), :]
+    ones = jnp.ones((chunk, HEAD_DIM), jnp.bfloat16)
+    top, total = (None, None)
+    for at in range(0, k_all.shape[0], chunk):
+        keys = k_all[at : at + chunk, :]
+        vals = jnp.concatenate([v_all[at : at + chunk, :], ones], axis=1)
+        scores = lax.dot_general(q, keys, NT, preferred_element_type=jnp.float32)
+        high = jnp.max(scores, axis=1, keepdims=True)
+        if top is not None:
+            high = jnp.maximum(top, high)
+        probs = jnp.exp2(scores - high).astype(jnp.bfloat16)
+        term = jnp.dot(probs, vals, preferred_element_type=jnp.float32)
+        total = term if top is None else total * jnp.exp2(top - high) + term
+        top = high
+    out_ref[...] = (total[:, :HEAD_DIM] / total[:, HEAD_DIM:]).astype(jnp.bfloat16)
+
+
+def attention(place, blocks, rows=1024, chunk=256):
+    tokens = sum(b.shape[1] for b in blocks)
+    whole = pl.BlockSpec(memory_space=pltpu.VMEM)
+    return pl.pallas_call(
+        functools.partial(attention_kernel, len(blocks), chunk),
+        grid_spec=pltpu.PrefetchScalarGridSpec(
+            num_scalar_prefetch=1,
+            grid=(tokens // rows,),
+            in_specs=[whole] * len(blocks),
+            out_specs=pl.BlockSpec((rows, HEAD_DIM), lambda i, s: (i, 0)),
+            scratch_shapes=[pltpu.VMEM((tokens, HEAD_DIM), jnp.bfloat16)] * 3,
+        ),
+        out_shape=jax.ShapeDtypeStruct((tokens, HEAD_DIM), jnp.bfloat16),
+        compiler_params=pltpu.CompilerParams(vmem_limit_bytes=VMEM_BYTES),
+        cost_estimate=pl.CostEstimate(
+            flops=tokens * tokens * HEAD_DIM * 4,
+            bytes_accessed=tokens * HEAD_DIM * 8,
+            transcendentals=tokens * tokens,
+        ),
+    )(place, *blocks)
 
 
 def padded_2(array, sides, width):
@@ -17,18 +162,6 @@
         after = lax.ppermute(initial, axis, down)
         array = jnp.concatenate([before, array, after], axis=dim)
     return array
-
-
-def local_attention(triple):
-    query = triple[0, :, 0:HEAD_DIM]
-    keys = triple[1, :, 0:HEAD_DIM]
-    vals = triple[2, :, 0:HEAD_DIM]
-    scores = jnp.dot(query, keys.T, preferred_element_type=jnp.float32) / jnp.sqrt(
-        jnp.float32(HEAD_DIM)
-    )
-    probs = jax.nn.softmax(scores, axis=-1).astype(jnp.bfloat16)
-    outputs = jnp.dot(probs, vals, preferred_element_type=jnp.float32).astype(jnp.bfloat16)
-    return outputs
 
 
 def update_rows(attended, noisy, w_out):
@@ -76,25 +209,64 @@
 def on_device(
     latent_tokens, modulation, w_qkv, w_out, noisy_latents, queue, frame_counts, conv_w, conv_b
 ):
+    z_low = lax.axis_index("group")
+    seat = lax.axis_index("seq")
+    y = lax.axis_index("dp")
+    x, z_high, core = (seat // 4, seat // 2 % 2, seat % 2)
+
+    quarter = w_qkv.shape[1] // 4
+    part = lax.dynamic_slice_in_dim(w_qkv, y * quarter, quarter, axis=1)
+    part_0 = moved(part, mirrored_z)
+    part_1 = moved(part_0, lambda x, y, z, core: (x, y - 1, z, core))
+    part_3 = moved(part_0, lambda x, y, z, core: (x, y + 1, z, core))
+    part_2 = moved(part_0, lambda x, y, z, core: (x, y + 2, z, core))
+    w_parts = (part_0, part_1, part_2, part_3)
+    parts = (y + jnp.arange(4, dtype=jnp.int32)) % 4
+
     values = latent_tokens[0].astype(jnp.float32)
     shift_scale = modulation[0]
     scaled = values * lax.rsqrt(jnp.mean(values * values, axis=-1, keepdims=True) + 1e-06)
     normed = (scaled * (1.0 + shift_scale[1]) + shift_scale[0]).astype(jnp.bfloat16)
-    projected = jnp.einsum(
-        "td,cdh->cth",
-        normed,
-        lax.all_gather(w_qkv, "seq", axis=2, tiled=True),
-        preferred_element_type=jnp.float32,
-    ).astype(jnp.bfloat16)
-    triple = lax.all_to_all(projected, "seq", split_axis=2, concat_axis=1, tiled=True)
-    head_outputs = local_attention(triple)
+
+    half = normed.shape[0] // 2
+    from_left = moved(normed, right)
+    from_right = moved(normed, left)
+    far_0 = moved(from_left[:half], right)
+    far_1 = moved(from_right[half:], left)
+    own_blocks = []
+    away_blocks = []
+    for tokens in ((normed,), (from_left,), (from_right,), (far_0, far_1)):
+        both = tokens + tuple(moved(t, other_core) for t in tokens)
+        own, away = project(parts, both, w_qkv, w_parts)
+        own_blocks.append(own)
+        away_blocks.append(moved(away, opposite_z))
+    places = []
+    for z_of in (z_high, 1 - z_high):
+        for step in (0, 3, 1, 2):
+            for core_of in (core, 1 - core):
+                places.append((((x + step) % XS) * 2 + z_of) * 2 + core_of)
+    place = jnp.stack(places).astype(jnp.int32)
+    head_outputs = attention(place, own_blocks + away_blocks)
+
     attended = lax.all_to_all(head_outputs, "seq", split_axis=0, concat_axis=1, tiled=True)
     new_latent = update_rows(attended, noisy_latents[0], w_out)[None]
-    slot_index = lax.axis_index(("group", "dp"))
+
+    slot_index = z_low * YS + y
     source = lax.dynamic_index_in_dim(queue, slot_index, 0, keepdims=False)
     limit = lax.dynamic_index_in_dim(frame_counts, source, 0, keepdims=False)
-    everyone = lax.all_gather(new_latent, ("group", "dp"), axis=0, tiled=True)
-    chosen = lax.dynamic_index_in_dim(everyone, source, 0, keepdims=False)
+    others = new_latent
+    others = jnp.concatenate(
+        [others, moved(others, lambda x, y, z, core: (x, y, z ^ 1, core))], axis=0
+    )
+    others = jnp.concatenate(
+        [others, moved(others, lambda x, y, z, core: (x, y ^ 1, z, core))], axis=0
+    )
+    others = jnp.concatenate(
+        [others, moved(others, lambda x, y, z, core: (x, y ^ 2, z, core))], axis=0
+    )
+    apart = source ^ slot_index
+    block = (apart // YS) + 2 * (apart % YS)
+    chosen = lax.dynamic_index_in_dim(others, block, 0, keepdims=False)
     padded = padded_2(chosen, (("seq", 2),), 1)
     decoded = causal_features(padded, limit, conv_w, conv_b)
     return (attended[None], decoded[None])

time: 483 us -> 215 us (0.45)
  waiting for transfers between devices: 252 us -> 71.9 us
  blocking collectives: 76.3 us -> 0 us
  matrix products: 71.1 us -> 3.98 us
  Pallas kernels: 0 us -> 44.4 us
  starting transfers between devices: 16.3 us -> 58 us
  other arithmetic: 25 us -> 6.48 us
  between operations: 16.3 us -> 3.73 us
    all_gather x1 -> x0, waiting for transfers between devices: 237 us -> none  [on_device(): lax.all_gather(w_qkv, 'seq', axis=2, tiled=True)]
    dot_general x3 -> x0, matrix products: 67.2 us -> none  [the longest x1 24.9 us: local_attention(): jnp.dot(probs, vals, preferred_element_type=jnp.float32)]
    ppermute x0 -> x20, waiting for transfers between devices: none -> 54.9 us  [moved(): return lax.ppermute(array, EVERY, perm)]
    all_to_all x1 -> x0, blocking collectives: 54.3 us -> none  [on_device(): lax.all_to_all(projected, 'seq', split_axis=2, concat_axis=1, tiled=True)]
    pallas_call x0 -> x5, Pallas kernels: none -> 44.4 us  [the longest x4 22.8 us: project(): pl.pallas_call(functools.partial(project_kernel, len(tokens)), grid_spec=...]
    ppermute x0 -> x20, starting transfers between devices: none -> 41.4 us  [moved(): return lax.ppermute(array, EVERY, perm)]
    all_gather x1 -> x0, blocking collectives: 22 us -> none  [on_device(): everyone = lax.all_gather(new_latent, ('group', 'dp'), axis=0, tiled=True)]
    reduce_sum x1 -> x0, other arithmetic: 21.5 us -> none  [local_attention(): probs = jax.nn.softmax(scores, axis=-1).astype(jnp.bfloat16)]
  transfers between devices with their start and end apart: 4 -> 23, of which waited for: 2 -> 9; matrix products, arithmetic and copies ran while one was open for 1% -> 4% of each run, Pallas kernels for 0% -> 11%
where the time goes in v1:
time: 215 us; the launch traced here: 214 us
  waiting for transfers between devices  71.9 us (33%)
  starting transfers between devices  58 us (27%)
  Pallas kernels  44.4 us (21%)
  local copies, waits for them, and re-layouts  25.4 us (12%)
  other arithmetic  6.48 us (3%)
  matrix products  3.98 us (2%)
  between operations  3.73 us (2%)
    ppermute x20, waiting for transfers between devices, moved(): return lax.ppermute(array, EVERY, perm)  54.9 us
    ppermute x20, starting transfers between devices, moved(): return lax.ppermute(array, EVERY, perm)  41.4 us
    pallas_call x4, Pallas kernels, project(): pl.pallas_call(functools.partial(project_kernel, len(tokens)), grid_spec=...  22.8 us
    pallas_call x1, Pallas kernels, attention(): pl.pallas_call(functools.partial(attention_kernel, len(blocks), chunk), g...  21.6 us
    all_to_all x1, waiting for transfers between devices, on_device(): lax.all_to_all(head_outputs, 'seq', split_axis=0, concat_axis=1, tiled=True)  17 us
    unnamed x62, local copies, waits for them, and re-layouts  11.4 us
    all_to_all x1, starting transfers between devices, on_device(): lax.all_to_all(head_outputs, 'seq', split_axis=0, concat_axis=1, tiled=True)  8.32 us
    ppermute x1, starting transfers between devices, padded_2(): after = lax.ppermute(initial, axis, down)  6.02 us
  transfers between devices with their start and end apart: 23, of which 9 were waited for; matrix products, arithmetic and copies ran while one was open for 4% of the time, Pallas kernels for 11%

profile of v1, /device:TPU:1, one launch (start us, length us, event | category | flops | bytes accessed | tf_op | source)
XLA Modules:
  0.0 213.9 jit_solution(7645575623470322753)
XLA Ops:
  4.0 2.1 collective-permute-start.5
  8.5 4.0 %collective-permute-start.1 = (bf16[3,768,128]{2,1,0:T(8,128)(2,1)S(1)}, bf16[3,768,128]{2,1,0:T(8,128)(2,1)S(1)}, u32[]{:S(2)}, u32[]{:S(2)}) collective-permute-start(bf16[3,768,128]{2,1,0:T(8,128)(2,1)S(1)} %constant_dynamic-slice_fusion), channel_id=1, source_target_pairs={{0,72},{4,76},{64,8},{68,12},{8,64},{12,68},{72,0},{76,4},{1,73},{... | collective-permute-start | bytes 1769480 | tf_op jit(solution)/shard_map/ppermute | solution.py:32
  12.5 12.5 %collective-permute-done.1.refs_3_.refs_5_ = bf16[3,768,128]{2,1,0:T(8,128)(2,1)S(1)} collective-permute-done((bf16[3,768,128]{2,1,0:T(8,128)(2,1)S(1)}, bf16[3,768,128]{2,1,0:T(8,128)(2,1)S(1)}, u32[]{:S(2)}, u32[]{:S(2)}) %collective-permute-start.1) | collective-permute-done | bytes 589856 | tf_op jit(solution)/shard_map/ppermute | solution.py:32
  25.0 2.7 %collective-permute-start.2 = (bf16[3,768,128]{2,1,0:T(8,128)(2,1)S(1)}, bf16[3,768,128]{2,1,0:T(8,128)(2,1)S(1)}, u32[]{:S(2)}, u32[]{:S(2)}) collective-permute-start(bf16[3,768,128]{2,1,0:T(8,128)(2,1)S(1)} %collective-permute-done.1.refs_3_.refs_5_), channel_id=1, source_target_pairs={{0,3},{4,7},{64,67},{68,71},{8,11},{12,15},{72,75},{76,79},{1,0},{... | collective-permute-start | bytes 1769480 | tf_op jit(solution)/shard_map/ppermute | solution.py:32
  27.8 2.0 collective-permute-start
  30.1 9.5 %collective-permute-done.2.refs_4_.refs_6_ = bf16[3,768,128]{2,1,0:T(8,128)(2,1)S(1)} collective-permute-done((bf16[3,768,128]{2,1,0:T(8,128)(2,1)S(1)}, bf16[3,768,128]{2,1,0:T(8,128)(2,1)S(1)}, u32[]{:S(2)}, u32[]{:S(2)}) %collective-permute-start.2) | collective-permute-done | bytes 589856 | tf_op jit(solution)/shard_map/ppermute | solution.py:32
  41.1 12.8 %collective-permute-start.6 = (bf16[256,3072]{1,0:T(8,128)(2,1)}, bf16[256,3072]{1,0:T(8,128)(2,1)S(1)}, u32[]{:S(2)}, u32[]{:S(2)}) collective-permute-start(bf16[256,3072]{1,0:T(8,128)(2,1)} %collective-permute-done.5.refs_0_), channel_id=1, source_target_pairs={{0,4},{4,0},{64,68},{68,64},{8,12},{12,8},{72,76},{76,72},{1,5},{5... | collective-permute-start | bytes 4718600 | tf_op jit(solution)/shard_map/ppermute | solution.py:32
  56.5 2.7 %collective-permute-start.10 = (bf16[128,3072]{1,0:T(8,128)(2,1)S(1)}, bf16[128,3072]{1,0:T(8,128)(2,1)S(1)}, u32[]{:S(2)}, u32[]{:S(2)}) collective-permute-start(bf16[128,3072]{1,0:T(8,128)(2,1)S(1)} %slice.153), channel_id=1, source_target_pairs={{0,48},{4,52},{64,112},{68,116},{8,56},{12,60},{72,120},{76,124},{... | collective-permute-start | bytes 2359304 | tf_op jit(solution)/shard_map/ppermute | solution.py:32
  59.2 17.2 %collective-permute-done.9.refs_0_ = bf16[128,3072]{1,0:T(8,128)(2,1)S(1)} collective-permute-done((bf16[128,3072]{1,0:T(8,128)(2,1)S(1)}, bf16[128,3072]{1,0:T(8,128)(2,1)S(1)}, u32[]{:S(2)}, u32[]{:S(2)}) %collective-permute-start.9) | collective-permute-done | bytes 786464 | tf_op jit(solution)/shard_map/ppermute | solution.py:32
  78.8 5.4 %shard_map.104 = (bf16[3,512,128]{2,1,0:T(8,128)(2,1)S(1)}, bf16[3,512,128]{2,1,0:T(8,128)(2,1)S(1)}) custom-call(s32[4]{0:T(128)S(1)} %and_select_fusion.part_ref, bf16[256,3072]{1,0:T(8,128)(2,1)S(1)} %fusion.3.refs_0_, bf16[256,3072]{1,0:T(8,128)(2,1)} %copy-done.12, bf16[3,3072,128]{2,1,0:T(8,128)(2,1)} %refs_4_.1, ...), custom_call_target="tpu_custom_call" | custom-call | flops 2415919104 | bytes 7864320 | tf_op jit(solution)/shard_map/pallas_call | solution.py:79
  86.5 5.8 %shard_map.105 = (bf16[3,512,128]{2,1,0:T(8,128)(2,1)S(1)}, bf16[3,512,128]{2,1,0:T(8,128)(2,1)S(1)}) custom-call(s32[4]{0:T(128)S(1)} %and_select_fusion.part_ref, bf16[256,3072]{1,0:T(8,128)(2,1)} %collective-permute-done.5.refs_0_, bf16[256,3072]{1,0:T(8,128)(2,1)} %copy-done.14, bf16[3,3072,128]{2,1,0:T(8,128)(2,1)} %refs_4_.1, ...), custom_call_target="tpu_custom_call" | custom-call | flops 2415919104 | bytes 7864320 | tf_op jit(solution)/shard_map/pallas_call | solution.py:79
  96.2 5.8 %shard_map.106 = (bf16[3,512,128]{2,1,0:T(8,128)(2,1)S(1)}, bf16[3,512,128]{2,1,0:T(8,128)(2,1)S(1)}) custom-call(s32[4]{0:T(128)S(1)} %and_select_fusion.part_ref, bf16[256,3072]{1,0:T(8,128)(2,1)} %collective-permute-done.7.refs_0_, bf16[256,3072]{1,0:T(8,128)(2,1)} %copy-done.13, bf16[3,3072,128]{2,1,0:T(8,128)(2,1)} %refs_4_.1, ...), custom_call_target="tpu_custom_call" | custom-call | flops 2415919104 | bytes 7864320 | tf_op jit(solution)/shard_map/pallas_call | solution.py:79
  104.0 5.8 %shard_map.107 = (bf16[3,512,128]{2,1,0:T(8,128)(2,1)S(1)}, bf16[3,512,128]{2,1,0:T(8,128)(2,1)}) custom-call(s32[4]{0:T(128)S(1)} %and_select_fusion.part_ref, bf16[128,3072]{1,0:T(8,128)(2,1)S(1)} %collective-permute-done.9.refs_0_, bf16[128,3072]{1,0:T(8,128)(2,1)S(1)} %collective-permute-done.10.refs_1_, ...), custom_call_target="tpu_custom_call" | custom-call | flops 2415919104 | bytes 7864320 | tf_op jit(solution)/shard_map/pallas_call | solution.py:79
  113.2 8.5 %collective-permute-done.16.refs_7_ = bf16[3,512,128]{2,1,0:T(8,128)(2,1)} collective-permute-done((bf16[3,512,128]{2,1,0:T(8,128)(2,1)}, bf16[3,512,128]{2,1,0:T(8,128)(2,1)}, u32[]{:S(2)}, u32[]{:S(2)}) %collective-permute-start.16) | collective-permute-done | bytes 393248 | tf_op jit(solution)/shard_map/ppermute | solution.py:32
  125.6 21.6 %shard_map.108 = bf16[4096,128]{1,0:T(8,128)(2,1)} custom-call(s32[16]{0:T(128)S(1)} %stack.149.place_ref, bf16[3,512,128]{2,1,0:T(8,128)(2,1)S(1)} %copy-done.2, bf16[3,512,128]{2,1,0:T(8,128)(2,1)S(1)} %copy-done.4, bf16[3,512,128]{2,1,0:T(8,128)(2,1)S(1)} %copy-done.6, bf16[3,512,128]{2,1,0:T(8,128)(2,1)S(1)} %copy-done.8, ...), custom_call_target="tpu_custom_call" | custom-call | flops 8589934592 | bytes 4194304 | tf_op jit(solution)/shard_map/pallas_call | solution.py:135
  147.2 8.3 %all-to-all-start = ((bf16[16,256,128]{2,1,0:T(8,128)(2,1)}), bf16[16,256,128]{2,1,0:T(8,128)(2,1)S(1)}, u32[]{:S(2)}, u32[]{:S(2)}) async-start(bf16[16,256,128]{2,1,0:T(8,128)(2,1)} %bitcast.20), calls=%async_computation | async-start | bytes 2097152 | tf_op jit(solution)/shard_map/all_to_all | solution.py:251
  155.7 17.0 %all-to-all-done = bf16[16,256,128]{2,1,0:T(8,128)(2,1)S(1)} async-done(((bf16[16,256,128]{2,1,0:T(8,128)(2,1)}), bf16[16,256,128]{2,1,0:T(8,128)(2,1)S(1)}, u32[]{:S(2)}, u32[]{:S(2)}) %all-to-all-start) | async-done | bytes 1048608 | tf_op jit(solution)/shard_map/all_to_all | solution.py:251
  178.5 2.0 collective-permute-done.17
  180.6 3.1 %collective-permute-done.18 = bf16[2,16,4,2,128]{4,1,3,2,0:T(8,128)(2,1)S(1)} collective-permute-done((bf16[2,16,4,2,128]{4,1,3,2,0:T(8,128)(2,1)S(1)}, bf16[2,16,4,2,128]{4,1,3,2,0:T(8,128)(2,1)S(1)}, u32[]{:S(2)}, u32[]{:S(2)}) %collective-permute-start.18) | collective-permute-done | bytes 65568 | tf_op jit(solution)/shard_map/ppermute | solution.py:32
  183.7 5.0 %collective-permute-start.19 = (bf16[4,16,4,2,128]{4,1,3,2,0:T(8,128)(2,1)S(1)}, bf16[4,16,4,2,128]{4,1,3,2,0:T(8,128)(2,1)S(1)}, u32[]{:S(2)}, u32[]{:S(2)}) collective-permute-start(bf16[4,16,4,2,128]{4,1,3,2,0:T(8,128)(2,1)S(1)} %pad_maximum_fusion), channel_id=1, source_target_pairs={{0,2},{4,6},{64,66},{68,70},{8,10},{12,14},{72,74},{76,78},{1,3},{... | collective-permute-start | bytes 393224 | tf_op jit(solution)/shard_map/ppermute | solution.py:32
  192.6 6.0 %collective-permute-start.21 = (bf16[16,4,1,128]{3,0,2,1:T(8,128)(2,1)S(1)}, bf16[16,4,1,128]{3,0,2,1:T(8,128)(2,1)S(1)}, u32[]{:S(2)}, u32[]{:S(2)}) collective-permute-start(bf16[16,4,1,128]{3,0,2,1:T(8,128)(2,1)S(1)} %get-tuple-element.19), channel_id=1, source_target_pairs={{4,0},{8,4},{12,8},{16,12},{20,16},{24,20},{28,24},{32,28},{36,32}... | collective-permute-start | bytes 49160 | tf_op jit(solution)/shard_map/ppermute | solution.py:162
  198.6 2.2 %collective-permute-start.20 = (bf16[16,4,1,128]{3,0,2,1:T(8,128)(2,1)S(1)}, bf16[16,4,1,128]{3,0,2,1:T(8,128)(2,1)S(1)}, u32[]{:S(2)}, u32[]{:S(2)}) collective-permute-start(bf16[16,4,1,128]{3,0,2,1:T(8,128)(2,1)S(1)} %get-tuple-element.18), channel_id=1, source_target_pairs={{0,4},{4,8},{8,12},{12,16},{16,20},{20,24},{24,28},{28,32},{32,36}... | collective-permute-start | bytes 49160 | tf_op jit(solution)/shard_map/ppermute | solution.py:161
  206.9 2.1 convolution_add_fusion
  209.0 3.2 %copy.48 = f32[1,512,4,2,128]{4,3,2,1,0:T(2,128)S(1)} copy(f32[1,512,4,2,128]{1,4,3,2,0:T(8,128)} %bitcast.158) | data formatting | bytes 4194304 | tf_op jit(solution)/shard_map/reshape | solution.py:203
  (128 shorter events, 42.9 us)
Async XLA Ops:
  0.6 206.2 %copy-start = (bf16[512,432]{0,1:T(8,128)(2,1)S(1)}, bf16[512,432]{0,1:T(8,128)(2,1)}, u32[]{:S(2)}) copy-start(bf16[512,432]{0,1:T(8,128)(2,1)} %param.16) | copy-start | bytes 1327108
  4.0 37.2 %collective-permute-start.5 = (bf16[256,3072]{1,0:T(8,128)(2,1)S(1)}, bf16[256,3072]{1,0:T(8,128)(2,1)}, u32[]{:S(2)}, u32[]{:S(2)}) collective-permute-start(bf16[256,3072]{1,0:T(8,128)(2,1)S(1)} %fusion.3.refs_0_), channel_id=1, source_target_pairs={{0,16},{4,20},{64,80},{68,84},{8,24},{12,28},{72,88},{76,92},{1,17... | collective-permute-start | bytes 4718600 | tf_op jit(solution)/shard_map/ppermute | solution.py:32
  6.1 47.9 %collective-permute-start.7 = (bf16[256,3072]{1,0:T(8,128)(2,1)S(1)}, bf16[256,3072]{1,0:T(8,128)(2,1)}, u32[]{:S(2)}, u32[]{:S(2)}) collective-permute-start(bf16[256,3072]{1,0:T(8,128)(2,1)S(1)} %fusion.3.refs_0_), channel_id=1, source_target_pairs={{0,48},{4,52},{64,112},{68,116},{8,56},{12,60},{72,120},{76,124},{... | collective-permute-start | bytes 4718600 | tf_op jit(solution)/shard_map/ppermute | solution.py:32
  8.5 16.5 %collective-permute-start.1 = (bf16[3,768,128]{2,1,0:T(8,128)(2,1)S(1)}, bf16[3,768,128]{2,1,0:T(8,128)(2,1)S(1)}, u32[]{:S(2)}, u32[]{:S(2)}) collective-permute-start(bf16[3,768,128]{2,1,0:T(8,128)(2,1)S(1)} %constant_dynamic-slice_fusion), channel_id=1, source_target_pairs={{0,72},{4,76},{64,8},{68,12},{8,64},{12,68},{72,0},{76,4},{1,73},{... | collective-permute-start | bytes 1769480 | tf_op jit(solution)/shard_map/ppermute | solution.py:32
  25.0 14.6 %collective-permute-start.2 = (bf16[3,768,128]{2,1,0:T(8,128)(2,1)S(1)}, bf16[3,768,128]{2,1,0:T(8,128)(2,1)S(1)}, u32[]{:S(2)}, u32[]{:S(2)}) collective-permute-start(bf16[3,768,128]{2,1,0:T(8,128)(2,1)S(1)} %collective-permute-done.1.refs_3_.refs_5_), channel_id=1, source_target_pairs={{0,3},{4,7},{64,67},{68,71},{8,11},{12,15},{72,75},{76,79},{1,0},{... | collective-permute-start | bytes 1769480 | tf_op jit(solution)/shard_map/ppermute | solution.py:32
  27.8 49.9 %collective-permute-start = (bf16[256,3072]{1,0:T(8,128)(2,1)S(1)}, bf16[256,3072]{1,0:T(8,128)(2,1)S(1)}, u32[]{:S(2)}, u32[]{:S(2)}) collective-permute-start(bf16[256,3072]{1,0:T(8,128)(2,1)S(1)} %fusion.3.refs_0_), channel_id=1, source_target_pairs={{0,4},{4,0},{64,68},{68,64},{8,12},{12,8},{72,76},{76,72},{1,5},{5... | collective-permute-start | bytes 4718600 | tf_op jit(solution)/shard_map/ppermute | solution.py:32
  29.8 26.6 %collective-permute-start.3 = (bf16[3,768,128]{2,1,0:T(8,128)(2,1)S(1)}, bf16[3,768,128]{2,1,0:T(8,128)(2,1)S(1)}, u32[]{:S(2)}, u32[]{:S(2)}) collective-permute-start(bf16[3,768,128]{2,1,0:T(8,128)(2,1)S(1)} %collective-permute-done.1.refs_3_.refs_5_), channel_id=1, source_target_pairs={{0,2},{4,6},{64,66},{68,70},{8,10},{12,14},{72,74},{76,78},{1,3},{... | collective-permute-start | bytes 1769480 | tf_op jit(solution)/shard_map/ppermute | solution.py:32
  39.7 16.8 %collective-permute-start.4 = (bf16[3,768,128]{2,1,0:T(8,128)(2,1)S(1)}, bf16[3,768,128]{2,1,0:T(8,128)(2,1)S(1)}, u32[]{:S(2)}, u32[]{:S(2)}) collective-permute-start(bf16[3,768,128]{2,1,0:T(8,128)(2,1)S(1)} %collective-permute-done.1.refs_3_.refs_5_), channel_id=1, source_target_pairs={{0,1},{4,5},{64,65},{68,69},{8,9},{12,13},{72,73},{76,77},{1,2},{5... | collective-permute-start | bytes 1769480 | tf_op jit(solution)/shard_map/ppermute | solution.py:32
  41.1 44.2 %collective-permute-start.6 = (bf16[256,3072]{1,0:T(8,128)(2,1)}, bf16[256,3072]{1,0:T(8,128)(2,1)S(1)}, u32[]{:S(2)}, u32[]{:S(2)}) collective-permute-start(bf16[256,3072]{1,0:T(8,128)(2,1)} %collective-permute-done.5.refs_0_), channel_id=1, source_target_pairs={{0,4},{4,0},{64,68},{68,64},{8,12},{12,8},{72,76},{76,72},{1,5},{5... | collective-permute-start | bytes 4718600 | tf_op jit(solution)/shard_map/ppermute | solution.py:32
  53.9 41.1 %collective-permute-start.8 = (bf16[256,3072]{1,0:T(8,128)(2,1)}, bf16[256,3072]{1,0:T(8,128)(2,1)S(1)}, u32[]{:S(2)}, u32[]{:S(2)}) collective-permute-start(bf16[256,3072]{1,0:T(8,128)(2,1)} %collective-permute-done.7.refs_0_), channel_id=1, source_target_pairs={{0,4},{4,0},{64,68},{68,64},{8,12},{12,8},{72,76},{76,72},{1,5},{5... | collective-permute-start | bytes 4718600 | tf_op jit(solution)/shard_map/ppermute | solution.py:32
  56.4 20.0 %collective-permute-start.9 = (bf16[128,3072]{1,0:T(8,128)(2,1)S(1)}, bf16[128,3072]{1,0:T(8,128)(2,1)S(1)}, u32[]{:S(2)}, u32[]{:S(2)}) collective-permute-start(bf16[128,3072]{1,0:T(8,128)(2,1)S(1)} %slice.152), channel_id=1, source_target_pairs={{0,16},{4,20},{64,80},{68,84},{8,24},{12,28},{72,88},{76,92},{1,17... | collective-permute-start | bytes 2359304 | tf_op jit(solution)/shard_map/ppermute | solution.py:32
  56.5 21.1 %collective-permute-start.10 = (bf16[128,3072]{1,0:T(8,128)(2,1)S(1)}, bf16[128,3072]{1,0:T(8,128)(2,1)S(1)}, u32[]{:S(2)}, u32[]{:S(2)}) collective-permute-start(bf16[128,3072]{1,0:T(8,128)(2,1)S(1)} %slice.153), channel_id=1, source_target_pairs={{0,48},{4,52},{64,112},{68,116},{8,56},{12,60},{72,120},{76,124},{... | collective-permute-start | bytes 2359304 | tf_op jit(solution)/shard_map/ppermute | solution.py:32
  76.4 26.7 %collective-permute-start.11 = (bf16[128,3072]{1,0:T(8,128)(2,1)S(1)}, bf16[128,3072]{1,0:T(8,128)(2,1)S(1)}, u32[]{:S(2)}, u32[]{:S(2)}) collective-permute-start(bf16[128,3072]{1,0:T(8,128)(2,1)S(1)} %collective-permute-done.9.refs_0_), channel_id=1, source_target_pairs={{0,4},{4,0},{64,68},{68,64},{8,12},{12,8},{72,76},{76,72},{1,5},{5... | collective-permute-start | bytes 2359304 | tf_op jit(solution)/shard_map/ppermute | solution.py:32
  77.7 25.5 %collective-permute-start.12 = (bf16[128,3072]{1,0:T(8,128)(2,1)S(1)}, bf16[128,3072]{1,0:T(8,128)(2,1)S(1)}, u32[]{:S(2)}, u32[]{:S(2)}) collective-permute-start(bf16[128,3072]{1,0:T(8,128)(2,1)S(1)} %collective-permute-done.10.refs_1_), channel_id=1, source_target_pairs={{0,4},{4,0},{64,68},{68,64},{8,12},{12,8},{72,76},{76,72},{1,5},{5... | collective-permute-start | bytes 2359304 | tf_op jit(solution)/shard_map/ppermute | solution.py:32
  84.2 28.4 %collective-permute-start.13 = (bf16[3,512,128]{2,1,0:T(8,128)(2,1)S(1)}, bf16[3,512,128]{2,1,0:T(8,128)(2,1)S(1)}, u32[]{:S(2)}, u32[]{:S(2)}) collective-permute-start(bf16[3,512,128]{2,1,0:T(8,128)(2,1)S(1)} %get-tuple-element.14), channel_id=1, source_target_pairs={{0,8},{4,12},{64,72},{68,76},{8,0},{12,4},{72,64},{76,68},{1,9},{5... | collective-permute-start | bytes 1179656 | tf_op jit(solution)/shard_map/ppermute | solution.py:32
  93.0 19.6 %collective-permute-start.14 = (bf16[3,512,128]{2,1,0:T(8,128)(2,1)S(1)}, bf16[3,512,128]{2,1,0:T(8,128)(2,1)S(1)}, u32[]{:S(2)}, u32[]{:S(2)}) collective-permute-start(bf16[3,512,128]{2,1,0:T(8,128)(2,1)S(1)} %get-tuple-element.15), channel_id=1, source_target_pairs={{0,8},{4,12},{64,72},{68,76},{8,0},{12,4},{72,64},{76,68},{1,9},{5... | collective-permute-start | bytes 1179656 | tf_op jit(solution)/shard_map/ppermute | solution.py:32
  102.0 11.1 %collective-permute-start.15 = (bf16[3,512,128]{2,1,0:T(8,128)(2,1)S(1)}, bf16[3,512,128]{2,1,0:T(8,128)(2,1)S(1)}, u32[]{:S(2)}, u32[]{:S(2)}) collective-permute-start(bf16[3,512,128]{2,1,0:T(8,128)(2,1)S(1)} %get-tuple-element.16), channel_id=1, source_target_pairs={{0,8},{4,12},{64,72},{68,76},{8,0},{12,4},{72,64},{76,68},{1,9},{5... | collective-permute-start | bytes 1179656 | tf_op jit(solution)/shard_map/ppermute | solution.py:32
  110.5 11.1 %collective-permute-start.16 = (bf16[3,512,128]{2,1,0:T(8,128)(2,1)}, bf16[3,512,128]{2,1,0:T(8,128)(2,1)}, u32[]{:S(2)}, u32[]{:S(2)}) collective-permute-start(bf16[3,512,128]{2,1,0:T(8,128)(2,1)} %get-tuple-element.17), channel_id=1, source_target_pairs={{0,8},{4,12},{64,72},{68,76},{8,0},{12,4},{72,64},{76,68},{1,9},{5... | collective-permute-start | bytes 1179656 | tf_op jit(solution)/shard_map/ppermute | solution.py:32
  147.2 25.5 %all-to-all-start = ((bf16[16,256,128]{2,1,0:T(8,128)(2,1)}), bf16[16,256,128]{2,1,0:T(8,128)(2,1)S(1)}, u32[]{:S(2)}, u32[]{:S(2)}) async-start(bf16[16,256,128]{2,1,0:T(8,128)(2,1)} %bitcast.20), calls=%async_computation | async-start | bytes 2097152 | tf_op jit(solution)/shard_map/all_to_all | solution.py:251
  177.7 2.8 %collective-permute-start.17 = (bf16[1,16,4,2,128]{4,1,3,2,0:T(8,128)(2,1)S(1)}, bf16[1,16,4,2,128]{4,1,3,2,0:T(8,128)(2,1)S(1)}, u32[]{:S(2)}, u32[]{:S(2)}) collective-permute-start(bf16[1,16,4,2,128]{4,1,3,2,0:T(8,128)(2,1)S(1)} %add_convert_fusion), channel_id=1, source_target_pairs={{0,64},{4,68},{64,0},{68,4},{8,72},{12,76},{72,8},{76,12},{1,65},{... | collective-permute-start | bytes 98312 | tf_op jit(solution)/shard_map/ppermute | solution.py:32
  180.5 3.2 %collective-permute-start.18 = (bf16[2,16,4,2,128]{4,1,3,2,0:T(8,128)(2,1)S(1)}, bf16[2,16,4,2,128]{4,1,3,2,0:T(8,128)(2,1)S(1)}, u32[]{:S(2)}, u32[]{:S(2)}) collective-permute-start(bf16[2,16,4,2,128]{4,1,3,2,0:T(8,128)(2,1)S(1)} %pad_maximum_fusion.1), channel_id=1, source_target_pairs={{0,1},{4,5},{64,65},{68,69},{8,9},{12,13},{72,73},{76,77},{1,0},{5... | collective-permute-start | bytes 196616 | tf_op jit(solution)/shard_map/ppermute | solution.py:32
  183.7 8.8 %collective-permute-start.19 = (bf16[4,16,4,2,128]{4,1,3,2,0:T(8,128)(2,1)S(1)}, bf16[4,16,4,2,128]{4,1,3,2,0:T(8,128)(2,1)S(1)}, u32[]{:S(2)}, u32[]{:S(2)}) collective-permute-start(bf16[4,16,4,2,128]{4,1,3,2,0:T(8,128)(2,1)S(1)} %pad_maximum_fusion), channel_id=1, source_target_pairs={{0,2},{4,6},{64,66},{68,70},{8,10},{12,14},{72,74},{76,78},{1,3},{... | collective-permute-start | bytes 393224 | tf_op jit(solution)/shard_map/ppermute | solution.py:32
  192.6 10.9 %collective-permute-start.21 = (bf16[16,4,1,128]{3,0,2,1:T(8,128)(2,1)S(1)}, bf16[16,4,1,128]{3,0,2,1:T(8,128)(2,1)S(1)}, u32[]{:S(2)}, u32[]{:S(2)}) collective-permute-start(bf16[16,4,1,128]{3,0,2,1:T(8,128)(2,1)S(1)} %get-tuple-element.19), channel_id=1, source_target_pairs={{4,0},{8,4},{12,8},{16,12},{20,16},{24,20},{28,24},{32,28},{36,32}... | collective-permute-start | bytes 49160 | tf_op jit(solution)/shard_map/ppermute | solution.py:162
  198.6 4.8 %collective-permute-start.20 = (bf16[16,4,1,128]{3,0,2,1:T(8,128)(2,1)S(1)}, bf16[16,4,1,128]{3,0,2,1:T(8,128)(2,1)S(1)}, u32[]{:S(2)}, u32[]{:S(2)}) collective-permute-start(bf16[16,4,1,128]{3,0,2,1:T(8,128)(2,1)S(1)} %get-tuple-element.18), channel_id=1, source_target_pairs={{0,4},{4,8},{8,12},{12,16},{16,20},{20,24},{24,28},{28,32},{32,36}... | collective-permute-start | bytes 49160 | tf_op jit(solution)/shard_map/ppermute | solution.py:161
  (18 other events, 72.2 us)

commit v2 on v1

v2 whole, which is shorter than its diff:
```python
import functools
import math

import jax
import jax.numpy as jnp
from jax import lax
from jax.experimental import pallas as pl
from jax.experimental.pallas import tpu as pltpu
from jax.sharding import PartitionSpec as P

HEAD_DIM = 128
EVERY = ("group", "seq", "dp")
XS, ZS, YS = (4, 4, 4)
VMEM_BYTES = 20 << 20
QUERY_SCALE = math.log2(math.e) / math.sqrt(HEAD_DIM)
NT = (((1,), (1,)), ((), ()))


def linear(x, y, z, core):
    return ((z % 2) * 16 + (x * 2 + z // 2) * 2 + core) * YS + y


def moved(array, move):
    perm = []
    for x in range(XS):
        for y in range(YS):
            for z in range(ZS):
                for core in range(2):
                    to = move(x, y, z, core)
                    there = linear(to[0] % XS, to[1] % YS, to[2] % ZS, to[3])
                    perm.append((linear(x, y, z, core), there))
    return lax.ppermute(array, EVERY, perm)


def right(x, y, z, core):
    return (x + 1, y, z, core)


def left(x, y, z, core):
    return (x - 1, y, z, core)


def other_core(x, y, z, core):
    return (x, y, z, 1 - core)


def opposite_z(x, y, z, core):
    return (x, y, z + 2, core)


def mirrored_z(x, y, z, core):
    return (x, y, 3 - z, core)


def project_kernel(n_tokens, part_ref, *refs):
    tokens = refs[:n_tokens]
    w_ref = refs[n_tokens]
    w_parts = refs[n_tokens + 1 : n_tokens + 5]
    own_ref, away_ref = refs[n_tokens + 5 :]
    for c in range(3):
        total = None
        for k in range(4):
            depth = w_parts[k].shape[1]
            at = pl.multiple_of(part_ref[k] * depth, depth)
            rows = jnp.concatenate([t[:, pl.ds(at, depth)] for t in tokens], axis=0)
            columns = jnp.concatenate([w_ref[c, pl.ds(at, depth), :], w_parts[k][c]], axis=1)
            term = jnp.dot(rows, columns, preferred_element_type=jnp.float32)
            total = term if total is None else total + term
        if c == 0:
            total = total * QUERY_SCALE
        total = total.astype(jnp.bfloat16)
        own_ref[c] = total[:, :HEAD_DIM]
        away_ref[c] = total[:, HEAD_DIM:]


def project(parts, tokens, w_qkv, w_parts):
    rows = sum(t.shape[0] for t in tokens)
    depth = w_qkv.shape[1]
    vmem = pl.BlockSpec(memory_space=pltpu.VMEM)
    out = jax.ShapeDtypeStruct((3, rows, HEAD_DIM), jnp.bfloat16)
    return pl.pallas_call(
        functools.partial(project_kernel, len(tokens)),
        in_specs=[pl.BlockSpec(memory_space=pltpu.SMEM)] + [vmem] * (len(tokens) + 5),
        out_specs=[vmem, vmem],
        out_shape=(out, out),
        compiler_params=pltpu.CompilerParams(vmem_limit_bytes=VMEM_BYTES),
        cost_estimate=pl.CostEstimate(
            flops=rows * depth * 6 * HEAD_DIM * 2,
            bytes_accessed=rows * depth * 2 + depth * 6 * HEAD_DIM * 2,
            transcendentals=0,
        ),
    )(parts, *tokens, w_qkv, *w_parts)


def attend(q, blocks, state, chunk=256):
    ones = jnp.ones((chunk, HEAD_DIM), jnp.bfloat16)
    for block in blocks:
        for at in range(0, block.shape[1], chunk):
            keys = block[1, at : at + chunk, :]
            vals = jnp.concatenate([block[2, at : at + chunk, :], ones], axis=1)
            scores = lax.dot_general(q, keys, NT, preferred_element_type=jnp.float32)
            high = jnp.max(scores, axis=1, keepdims=True)
            if state is not None:
                high = jnp.maximum(state[0], high)
            probs = jnp.exp2(scores - high).astype(jnp.bfloat16)
            term = jnp.dot(probs, vals, preferred_element_type=jnp.float32)
            if state is not None:
                term = state[1] * jnp.exp2(state[0] - high) + term
            state = (high, term)
    return state


def finished(state):
    total = state[1]
    return (total[:, :HEAD_DIM] / total[:, HEAD_DIM:]).astype(jnp.bfloat16)


def first_kernel(n_blocks, *refs):
    blocks = refs[:n_blocks]
    q_ref, top_ref, total_ref, q_all = refs[n_blocks:]

    @pl.when(pl.program_id(0) == 0)
    def _():
        for i, block in enumerate(blocks):
            q_all[i * block.shape[1] : (i + 1) * block.shape[1], :] = block[0]

    rows = q_ref.shape[0]
    q = q_all[pl.ds(pl.multiple_of(pl.program_id(0) * rows, rows), rows), :]
    top, total = attend(q, blocks, None)
    q_ref[...] = q
    top_ref[...] = jnp.broadcast_to(top, top_ref.shape)
    total_ref[...] = total


def last_kernel(n_blocks, tiles, place_ref, *refs):
    blocks = refs[:n_blocks]
    q_ref, top_ref, total_ref, out_ref = refs[n_blocks:]
    rows = blocks[0].shape[1]
    half = rows // 2
    step = half // 2

    def put(first, outputs):
        for at in range(0, outputs.shape[0], step):
            owner, inside = divmod(first + at, half)
            to = pl.multiple_of(place_ref[owner] * half + inside, step)
            out_ref[pl.ds(to, step), :] = outputs[at : at + step]

    known = q_ref.shape[0]
    tile = known // tiles
    for t in range(tiles):
        here = slice(t * tile, (t + 1) * tile)
        state = (top_ref[here, :][:, :1], total_ref[here, :])
        put(t * tile, finished(attend(q_ref[here, :], blocks[-1:], state)))
    put(known, finished(attend(blocks[-1][0], blocks, None)))


def attention(place, blocks):
    early = blocks[:-1]
    rows = blocks[0].shape[1]
    known = rows * len(early)
    tile = known // 4
    tokens = known + rows
    vmem = pl.BlockSpec(memory_space=pltpu.VMEM)

    def cost(queries, keys):
        return pl.CostEstimate(
            flops=queries * keys * HEAD_DIM * 4,
            bytes_accessed=tokens * HEAD_DIM * 8,
            transcendentals=queries * keys,
        )

    q, top, total = pl.pallas_call(
        functools.partial(first_kernel, len(early)),
        grid=(known // tile,),
        in_specs=[vmem] * len(early),
        out_specs=[
            pl.BlockSpec((tile, HEAD_DIM), lambda i: (i, 0)),
            pl.BlockSpec((tile, HEAD_DIM), lambda i: (i, 0)),
            pl.BlockSpec((tile, 2 * HEAD_DIM), lambda i: (i, 0)),
        ],
        out_shape=[
            jax.ShapeDtypeStruct((known, HEAD_DIM), jnp.bfloat16),
            jax.ShapeDtypeStruct((known, HEAD_DIM), jnp.float32),
            jax.ShapeDtypeStruct((known, 2 * HEAD_DIM), jnp.float32),
        ],
        scratch_shapes=[pltpu.VMEM((known, HEAD_DIM), jnp.bfloat16)],
        compiler_params=pltpu.CompilerParams(vmem_limit_bytes=VMEM_BYTES),
        cost_estimate=cost(known, known),
    )(*early)
    return pl.pallas_call(
        functools.partial(last_kernel, len(blocks), 4),
        in_specs=[pl.BlockSpec(memory_space=pltpu.SMEM)] + [vmem] * (len(blocks) + 3),
        out_specs=vmem,
        out_shape=jax.ShapeDtypeStruct((tokens, HEAD_DIM), jnp.bfloat16),
        compiler_params=pltpu.CompilerParams(vmem_limit_bytes=VMEM_BYTES),
        cost_estimate=cost(2 * rows, tokens),
    )(place, *blocks, q, top, total)


def update_kernel(att_ref, noisy_ref, w_ref, out_ref):
    heads, tokens, width = att_ref.shape
    squares = jnp.zeros((tokens, width), jnp.float32)
    for h in range(heads):
        values = att_ref[h].astype(jnp.float32)
        squares += values * values
    mean = jnp.sum(squares, axis=1, keepdims=True) / (heads * width)
    gain = lax.rsqrt(mean + 1e-06)
    predicted = jnp.zeros((w_ref.shape[0], tokens), jnp.float32)
    for h in range(heads):
        normed = (att_ref[h].astype(jnp.float32) * gain).astype(jnp.bfloat16)
        predicted += lax.dot_general(
            w_ref[:, h * width : (h + 1) * width], normed, NT, preferred_element_type=jnp.float32
        )
    half = predicted.shape[0] // 2
    both = jnp.concatenate([predicted[:half], predicted[half:]], axis=1)
    parts = []
    for _ in range(3):
        part = both.astype(jnp.bfloat16)
        both = both - part.astype(jnp.float32)
        parts.append(part)
    token = lax.broadcasted_iota(jnp.int32, (2 * tokens, 2 * tokens), 0)
    column = lax.broadcasted_iota(jnp.int32, (2 * tokens, 2 * tokens), 1)
    spread = jnp.where(token < tokens, 2 * token, 2 * token - 2 * tokens + 1) == column
    spread = jnp.where(spread, 1.0, 0.0).astype(jnp.bfloat16)
    grid = jnp.dot(jnp.concatenate(parts, axis=0), spread, preferred_element_type=jnp.float32)
    grid = grid[:half] + grid[half : 2 * half] + grid[2 * half :]
    channels = half // 2
    frames = 2 * tokens // 128
    for dy in range(2):
        for f in range(frames):
            at = (dy * frames + f) * channels
            rows = grid[dy * channels : (dy + 1) * channels, f * 128 : (f + 1) * 128]
            noisy = noisy_ref[at : at + channels, :].astype(jnp.float32)
            out_ref[at : at + channels, :] = (noisy + rows).astype(jnp.bfloat16)


def update_rows(by_head, noisy, w_out):
    channels, frames, rows, columns = noisy.shape
    noisy = noisy.transpose(2, 1, 0, 3).reshape(rows * frames * channels, columns)
    w_rows = w_out.T.reshape(channels, 2, 2, -1).transpose(2, 1, 0, 3).reshape(4 * channels, -1)
    return pl.pallas_call(
        update_kernel,
        in_specs=[pl.BlockSpec(memory_space=pltpu.VMEM)] * 3,
        out_specs=pl.BlockSpec(memory_space=pltpu.VMEM),
        out_shape=jax.ShapeDtypeStruct(noisy.shape, jnp.bfloat16),
        compiler_params=pltpu.CompilerParams(vmem_limit_bytes=VMEM_BYTES),
    )(by_head, noisy, w_rows)


def features_kernel(limit_ref, rows_ref, before_ref, after_ref, w_ref, b_ref, out_ref, taps):
    frames, channels = (4, 16)
    line = frames * channels
    four = jnp.concatenate([before_ref[...], rows_ref[...], after_ref[...]], axis=0)
    wide = four.astype(jnp.float32)
    lane = lax.broadcasted_iota(jnp.int32, wide.shape, 1)
    from_left = jnp.where(lane == 0, 0.0, pltpu.roll(wide, 1, 1)).astype(jnp.bfloat16)
    from_right = jnp.where(lane == 127, 0.0, pltpu.roll(wide, 127, 1)).astype(jnp.bfloat16)
    shifted = (from_left, four, from_right)
    for dt in range(3):
        for dh in range(3):
            for dw in range(3):
                tap = (dt * 3 + dh) * 3 + dw
                for f in range(frames):
                    for y in range(2):
                        at = (y + dh) * line + max(f + dt - 2, 0) * channels
                        block = (f * 2 + y) * 128
                        taps[tap * channels : (tap + 1) * channels, block : block + 128] = shifted[
                            dw
                        ][at : at + channels]
    features = lax.dot_general(
        w_ref[...], taps[...], (((0,), (0,)), ((), ())), preferred_element_type=jnp.float32
    )
    features = features + b_ref[...]
    frame = lax.broadcasted_iota(jnp.int32, features.shape, 1) // 256
    features = jnp.where(frame < limit_ref[0], features, 0.0)
    out_ref[...] = features.reshape(out_ref.shape).astype(jnp.bfloat16)


def causal_features(rows, before, after, limit, conv_w, conv_b):
    outputs, depth = conv_w.shape
    columns = rows.shape[1]
    vmem = pl.BlockSpec(memory_space=pltpu.VMEM)
    out = pl.pallas_call(
        features_kernel,
        in_specs=[pl.BlockSpec(memory_space=pltpu.SMEM)] + [vmem] * 5,
        out_specs=vmem,
        out_shape=jax.ShapeDtypeStruct((outputs, 8, columns), jnp.bfloat16),
        scratch_shapes=[pltpu.VMEM((depth, 8 * columns), jnp.bfloat16)],
        compiler_params=pltpu.CompilerParams(vmem_limit_bytes=VMEM_BYTES),
    )(limit[None], rows, before, after, conv_w.T, conv_b[:, None])
    return out.reshape(outputs, 4, 2, columns)


def on_device(
    latent_tokens, modulation, w_qkv, w_out, noisy_latents, queue, frame_counts, conv_w, conv_b
):
    z_low = lax.axis_index("group")
    seat = lax.axis_index("seq")
    y = lax.axis_index("dp")
    x, z_high, core = (seat // 4, seat // 2 % 2, seat % 2)

    quarter = w_qkv.shape[1] // 4
    part_0 = moved(lax.dynamic_slice_in_dim(w_qkv, y * quarter, quarter, axis=1), mirrored_z)
    part_2 = lax.dynamic_slice_in_dim(w_qkv, (y + 2) % 4 * quarter, quarter, axis=1)
    parts = (y + jnp.arange(4, dtype=jnp.int32)) % 4

    values = latent_tokens[0].astype(jnp.float32)
    shift_scale = modulation[0]
    scaled = values * lax.rsqrt(jnp.mean(values * values, axis=-1, keepdims=True) + 1e-06)
    normed = (scaled * (1.0 + shift_scale[1]) + shift_scale[0]).astype(jnp.bfloat16)

    half = normed.shape[0] // 2
    from_left = moved(normed, right)
    from_right = moved(normed, left)
    swapped = moved(normed, other_core)
    part_0, part_2, swapped = lax.optimization_barrier((part_0, part_2, swapped))
    part_1 = moved(part_0, lambda x, y, z, core: (x, y - 1, z, core))
    part_3 = moved(part_0, lambda x, y, z, core: (x, y + 1, z, core))
    part_2 = moved(part_2, mirrored_z)
    from_left, from_right, part_1, part_2, part_3 = lax.optimization_barrier(
        (from_left, from_right, part_1, part_2, part_3)
    )
    w_parts = (part_0, part_1, part_2, part_3)

    def projected(*both):
        own, away = project(parts, both, w_qkv, w_parts)
        return own, moved(away, opposite_z)

    far_0 = moved(from_left[:half], right)
    far_1 = moved(from_right[half:], left)
    blocks = [projected(normed, swapped)]
    blocks.append(projected(from_left, moved(from_left, other_core)))
    blocks.append(projected(from_right, moved(from_right, other_core)))
    far_0, far_1, blocks[0], blocks[1], own = lax.optimization_barrier(
        (far_0, far_1, blocks[0], blocks[1], blocks[2][0])
    )
    blocks[2] = (own, blocks[2][1])
    blocks.append(projected(far_0, far_1, moved(far_0, other_core), moved(far_1, other_core)))
    places = []
    for z_of in (z_high, 1 - z_high):
        for step in (0, 3, 1, 2):
            for core_of in (core, 1 - core):
                places.append((((x + step) % XS) * 2 + z_of) * 2 + core_of)
    place = jnp.stack(places).astype(jnp.int32)
    head_outputs = attention(place, [b[0] for b in blocks] + [b[1] for b in blocks])

    tokens = latent_tokens.shape[1]
    by_head = lax.all_to_all(
        head_outputs.reshape(-1, tokens, HEAD_DIM), "seq", split_axis=0, concat_axis=0, tiled=True
    )
    attended = by_head.transpose(1, 0, 2).reshape(1, tokens, -1)
    new_rows = update_rows(by_head, noisy_latents[0], w_out)

    slot_index = z_low * YS + y
    source = lax.dynamic_index_in_dim(queue, slot_index, 0, keepdims=False)
    limit = lax.dynamic_index_in_dim(frame_counts, source, 0, keepdims=False)
    everyone = lax.all_to_all(
        jnp.broadcast_to(new_rows, (2 * YS,) + new_rows.shape),
        ("group", "dp"),
        split_axis=0,
        concat_axis=0,
        tiled=True,
    )
    chosen = lax.dynamic_index_in_dim(everyone, source, 0, keepdims=False)
    line = chosen.shape[0] // 2
    seats = lax.axis_size("seq")
    up = [(i, i + 1) for i in range(seats - 1)]
    before = lax.ppermute(chosen[line:], "seq", up)
    after = lax.ppermute(chosen[:line], "seq", [(j, i) for i, j in up])
    decoded = causal_features(chosen, before, after, limit, conv_w, conv_b)
    return (attended, decoded[None])


def solution(mesh):
    return jax.shard_map(
        on_device,
        mesh=mesh,
        in_specs=(
            P(("group", "dp"), "seq", None),
            P(("group", "dp"), None, None),
            P(None, None, "seq"),
            P(),
            P(("group", "dp"), None, None, "seq", None),
            P(),
            P(),
            P(),
            P(),
        ),
        out_specs=(P(("group", "dp"), "seq", None), P(("group", "dp"), None, None, "seq", None)),
        check_vma=False,
    )
```

time: 215 us -> 167 us (0.78)
  starting transfers between devices: 58 us -> 39.5 us
  waiting for transfers between devices: 71.9 us -> 58.9 us
  local copies, waits for them, and re-layouts: 25.4 us -> 14.5 us
  matrix products: 3.98 us -> 0 us
  other arithmetic: 6.48 us -> 3.29 us
  Pallas kernels: 44.4 us -> 47.3 us
    ppermute x20 -> x17, waiting for transfers between devices: 54.9 us -> 36.5 us  [moved(): return lax.ppermute(array, EVERY, perm)]
    ppermute x20 -> x17, starting transfers between devices: 41.4 us -> 24.2 us  [moved(): return lax.ppermute(array, EVERY, perm)]
    ppermute x2, waiting for transfers between devices: 0.01 us -> 4.61 us  [the longest x1 4.6 us: on_device(): after = lax.ppermute(chosen[:line], 'seq', [(j, i) for i, j in up])]
    dot_general x2 -> x0, matrix products: 3.98 us -> none  [the longest x1 2.11 us: causal_features(): jnp.dot(conv_w, stacked, preferred_element_type=jnp.float32)]
    reshape x3 -> x2, local copies, waits for them, and re-layouts: 3.96 us -> 0.33 us  [update_rows(): w_out.T.reshape(channels, 2, 2, -1).transpose(2, 1, 0, 3)]
    pallas_call x5 -> x8, Pallas kernels: 44.4 us -> 47.3 us  [the longest x4 16.6 us: project(): pl.pallas_call(functools.partial(project_kernel, len(tokens)), in_specs=[...]
    convert_element_type x4 -> x0, other arithmetic: 2.76 us -> none  [the longest x1 1.76 us: causal_features(): return (features * keep[None, :, None, None]).astype(jnp.bfloat16)]
    unnamed x62 -> x51, local copies, waits for them, and re-layouts: 11.4 us -> 8.73 us
  transfers between devices with their start and end apart: 23 -> 21, of which waited for: 9 -> 10; matrix products, arithmetic and copies ran while one was open for 4% -> 4% of each run, Pallas kernels for 11% -> 20%
where the time goes in v2:
time: 167 us; the launch traced here: 166 us
  waiting for transfers between devices  58.9 us (35%)
  Pallas kernels  47.3 us (28%)
  starting transfers between devices  39.5 us (24%)
  local copies, waits for them, and re-layouts  14.5 us (9%)
  other arithmetic  3.29 us (2%)
  between operations  2.96 us (2%)
    ppermute x17, waiting for transfers between devices, moved(): return lax.ppermute(array, EVERY, perm)  36.5 us
    ppermute x17, starting transfers between devices, moved(): return lax.ppermute(array, EVERY, perm)  24.2 us
    all_to_all x1, waiting for transfers between devices, on_device(): lax.all_to_all(head_outputs.reshape(-1, tokens, HEAD_DIM), 'seq', split_a...  16.8 us
    pallas_call x4, Pallas kernels, project(): pl.pallas_call(functools.partial(project_kernel, len(tokens)), in_specs=[...  16.6 us
    pallas_call x1, Pallas kernels, attention(): pl.pallas_call(functools.partial(first_kernel, len(early)), grid=(known /...  16 us
    pallas_call x1, Pallas kernels, attention(): pl.pallas_call(functools.partial(last_kernel, len(blocks), 4), in_specs=[...  11 us
    unnamed x51, local copies, waits for them, and re-layouts  8.73 us
    all_to_all x1, starting transfers between devices, on_device(): lax.all_to_all(head_outputs.reshape(-1, tokens, HEAD_DIM), 'seq', split_a...  5.42 us
  transfers between devices with their start and end apart: 21, of which 10 were waited for; matrix products, arithmetic and copies ran while one was open for 4% of the time, Pallas kernels for 20%

profile of v2, /device:TPU:1, one launch (start us, length us, event | category | flops | bytes accessed | tf_op | source)
XLA Modules:
  0.0 166.3 jit_solution(14303393952000790172)
XLA Ops:
  9.6 3.9 %collective-permute-start.2 = (bf16[3,768,128]{2,1,0:T(8,128)(2,1)S(1)}, bf16[3,768,128]{2,1,0:T(8,128)(2,1)S(1)}, u32[]{:S(2)}, u32[]{:S(2)}) collective-permute-start(bf16[3,768,128]{2,1,0:T(8,128)(2,1)S(1)} %get-tuple-element.57), channel_id=1, source_target_pairs={{0,72},{4,76},{64,8},{68,12},{8,64},{12,68},{72,0},{76,4},{1,73},{... | collective-permute-start | bytes 1769480 | tf_op jit(solution)/shard_map/ppermute | solution.py:32
  13.5 13.1 %collective-permute-done.2.refs_3_.refs_5_ = bf16[3,768,128]{2,1,0:T(8,128)(2,1)S(1)} collective-permute-done((bf16[3,768,128]{2,1,0:T(8,128)(2,1)S(1)}, bf16[3,768,128]{2,1,0:T(8,128)(2,1)S(1)}, u32[]{:S(2)}, u32[]{:S(2)}) %collective-permute-start.2) | collective-permute-done | bytes 589856 | tf_op jit(solution)/shard_map/ppermute | solution.py:32
  26.6 2.7 %collective-permute-start.4 = (bf16[3,768,128]{2,1,0:T(8,128)(2,1)S(1)}, bf16[3,768,128]{2,1,0:T(8,128)(2,1)S(1)}, u32[]{:S(2)}, u32[]{:S(2)}) collective-permute-start(bf16[3,768,128]{2,1,0:T(8,128)(2,1)S(1)} %collective-permute-done.2.refs_3_.refs_5_), channel_id=1, source_target_pairs={{0,3},{4,7},{64,67},{68,71},{8,11},{12,15},{72,75},{76,79},{1,0},{... | collective-permute-start | bytes 1769480 | tf_op jit(solution)/shard_map/ppermute | solution.py:32
  29.4 2.4 %collective-permute-start.5 = (bf16[3,768,128]{2,1,0:T(8,128)(2,1)S(1)}, bf16[3,768,128]{2,1,0:T(8,128)(2,1)S(1)}, u32[]{:S(2)}, u32[]{:S(2)}) collective-permute-start(bf16[3,768,128]{2,1,0:T(8,128)(2,1)S(1)} %get-tuple-element.29), channel_id=1, source_target_pairs={{0,72},{4,76},{64,8},{68,12},{8,64},{12,68},{72,0},{76,4},{1,73},{... | collective-permute-start | bytes 1769480 | tf_op jit(solution)/shard_map/ppermute | solution.py:32
  31.7 10.9 %collective-permute-done.refs_0_ = bf16[256,3072]{1,0:T(8,128)(2,1)S(1)} collective-permute-done((bf16[256,3072]{1,0:T(8,128)(2,1)S(1)}, bf16[256,3072]{1,0:T(8,128)(2,1)S(1)}, u32[]{:S(2)}, u32[]{:S(2)}) %collective-permute-start) | collective-permute-done | bytes 1572896 | tf_op jit(solution)/shard_map/ppermute | solution.py:32
  45.7 3.0 %collective-permute-start.10 = (bf16[256,3072]{1,0:T(8,128)(2,1)S(1)}, bf16[256,3072]{1,0:T(8,128)(2,1)S(1)}, u32[]{:S(2)}, u32[]{:S(2)}) collective-permute-start(bf16[256,3072]{1,0:T(8,128)(2,1)S(1)} %collective-permute-done.refs_0_), channel_id=1, source_target_pairs={{0,4},{4,0},{64,68},{68,64},{8,12},{12,8},{72,76},{76,72},{1,5},{5... | collective-permute-start | bytes 4718600 | tf_op jit(solution)/shard_map/ppermute | solution.py:32
  50.0 2.7 %collective-permute-start.8 = (bf16[128,3072]{1,0:T(8,128)(2,1)S(1)}, bf16[128,3072]{1,0:T(8,128)(2,1)}, u32[]{:S(2)}, u32[]{:S(2)}) collective-permute-start(bf16[128,3072]{1,0:T(8,128)(2,1)S(1)} %slice.29), channel_id=1, source_target_pairs={{0,48},{4,52},{64,112},{68,116},{8,56},{12,60},{72,120},{76,124},{... | collective-permute-start | bytes 2359304 | tf_op jit(solution)/shard_map/ppermute | solution.py:32
  52.7 4.1 %shard_map.104 = (bf16[3,512,128]{2,1,0:T(8,128)(2,1)S(1)}, bf16[3,512,128]{2,1,0:T(8,128)(2,1)S(1)}) custom-call(s32[4]{0:T(128)S(1)} %and_select_fusion.part_ref, bf16[256,3072]{1,0:T(8,128)(2,1)S(1)} %fusion.3.refs_0_, bf16[256,3072]{1,0:T(8,128)(2,1)} %collective-permute-done.3.refs_1_, bf16[3,3072,128]{2,1,0:T(8,128)(2,1)S(1)} %copy-done, ...), custom_call_target="tpu_custom_call" | custom-call | flops 2415919104 | bytes 7864320 | tf_op jit(solution)/shard_map/pallas_call | solution.py:81
  56.9 3.2 %shard_map.105 = (bf16[3,512,128]{2,1,0:T(8,128)(2,1)S(1)}, bf16[3,512,128]{2,1,0:T(8,128)(2,1)S(1)}) custom-call(s32[4]{0:T(128)S(1)} %and_select_fusion.part_ref, bf16[256,3072]{1,0:T(8,128)(2,1)S(1)} %collective-permute-done.refs_0_, bf16[256,3072]{1,0:T(8,128)(2,1)S(1)} %collective-permute-done.10.refs_1_, bf16[3,3072,128]{2,1,0:T(8,128)(2,1)S(1)} %copy-done, ...), custom_call_target="tpu_custom_call" | custom-call | flops 2415919104 | bytes 7864320 | tf_op jit(solution)/shard_map/pallas_call | solution.py:81
  60.8 2.9 %collective-permute-start.11 = (bf16[3,512,128]{2,1,0:T(8,128)(2,1)S(1)}, bf16[3,512,128]{2,1,0:T(8,128)(2,1)S(1)}, u32[]{:S(2)}, u32[]{:S(2)}) collective-permute-start(bf16[3,512,128]{2,1,0:T(8,128)(2,1)S(1)} %get-tuple-element.39), channel_id=1, source_target_pairs={{0,8},{4,12},{64,72},{68,76},{8,0},{12,4},{72,64},{76,68},{1,9},{5... | collective-permute-start | bytes 1179656 | tf_op jit(solution)/shard_map/ppermute | solution.py:32
  63.8 4.8 %shard_map.106 = (bf16[3,512,128]{2,1,0:T(8,128)(2,1)S(1)}, bf16[3,512,128]{2,1,0:T(8,128)(2,1)}) custom-call(s32[4]{0:T(128)S(1)} %and_select_fusion.part_ref, bf16[256,3072]{1,0:T(8,128)(2,1)} %collective-permute-done.1.refs_0_, bf16[256,3072]{1,0:T(8,128)(2,1)S(1)} %collective-permute-done.12.refs_1_, bf16[3,3072,128]{2,1,0:T(8,128)(2,1)S(1)} %copy-done, ...), custom_call_target="tpu_custom_call" | custom-call | flops 2415919104 | bytes 7864320 | tf_op jit(solution)/shard_map/pallas_call | solution.py:81
  70.1 6.2 %collective-permute-done.11.refs_5_ = bf16[3,512,128]{2,1,0:T(8,128)(2,1)S(1)} collective-permute-done((bf16[3,512,128]{2,1,0:T(8,128)(2,1)S(1)}, bf16[3,512,128]{2,1,0:T(8,128)(2,1)S(1)}, u32[]{:S(2)}, u32[]{:S(2)}) %collective-permute-start.11) | collective-permute-done | bytes 393248 | tf_op jit(solution)/shard_map/ppermute | solution.py:32
  77.0 2.0 %collective-permute-start.13 = (bf16[128,3072]{1,0:T(8,128)(2,1)}, bf16[128,3072]{1,0:T(8,128)(2,1)}, u32[]{:S(2)}, u32[]{:S(2)}) collective-permute-start(bf16[128,3072]{1,0:T(8,128)(2,1)} %collective-permute-done.7.refs_0_), channel_id=1, source_target_pairs={{0,4},{4,0},{64,68},{68,64},{8,12},{12,8},{72,76},{76,72},{1,5},{5... | collective-permute-start | bytes 2359304 | tf_op jit(solution)/shard_map/ppermute | solution.py:32
  79.2 2.1 %collective-permute-done.13.refs_2_ = bf16[128,3072]{1,0:T(8,128)(2,1)} collective-permute-done((bf16[128,3072]{1,0:T(8,128)(2,1)}, bf16[128,3072]{1,0:T(8,128)(2,1)}, u32[]{:S(2)}, u32[]{:S(2)}) %collective-permute-start.13) | collective-permute-done | bytes 786464 | tf_op jit(solution)/shard_map/ppermute | solution.py:32
  86.7 4.5 %shard_map.107 = (bf16[3,512,128]{2,1,0:T(8,128)(2,1)S(1)}, bf16[3,512,128]{2,1,0:T(8,128)(2,1)S(1)}) custom-call(s32[4]{0:T(128)S(1)} %and_select_fusion.part_ref, bf16[128,3072]{1,0:T(8,128)(2,1)} %collective-permute-done.7.refs_0_, bf16[128,3072]{1,0:T(8,128)(2,1)} %collective-permute-done.8.refs_1_, bf16[128,3072]{1,0:T(8,128)(2,1)} %collective-permute-done.13.refs_2_, ...), custom_call_target="tpu_custom_call" | custom-call | flops 2415919104 | bytes 7864320 | tf_op jit(solution)/shard_map/pallas_call | solution.py:81
  91.4 16.0 %shard_map.108 = (bf16[3584,128]{1,0:T(8,128)(2,1)S(1)}, f32[3584,128]{1,0:T(8,128)S(1)}, f32[3584,256]{1,0:T(8,128)S(1)}) custom-call(bf16[3,512,128]{2,1,0:T(8,128)(2,1)S(1)} %get-tuple-element.41.refs_0_, bf16[3,512,128]{2,1,0:T(8,128)(2,1)S(1)} %copy-done.6, bf16[3,512,128]{2,1,0:T(8,128)(2,1)S(1)} %copy-done.10, ...), custom_call_target="tpu_custom_call" | custom-call | flops 6576668672 | bytes 4194304 | tf_op jit(solution)/shard_map/pallas_call | solution.py:172
  107.5 11.0 %shard_map.109 = bf16[4096,128]{1,0:T(8,128)(2,1)} custom-call(s32[16]{0:T(128)S(1)} %stack.67.place_ref, bf16[3,512,128]{2,1,0:T(8,128)(2,1)S(1)} %get-tuple-element.41.refs_0_, bf16[3,512,128]{2,1,0:T(8,128)(2,1)S(1)} %copy-done.6, bf16[3,512,128]{2,1,0:T(8,128)(2,1)S(1)} %copy-done.10, bf16[3,512,128]{2,1,0:T(8,128)(2,1)S(1)} %get-tuple-element.46.refs_3_, ...), custom_call_target="tpu_custom_call" | custom-call | flops 2147483648 | bytes 4194304 | tf_op jit(solution)/shard_map/pallas_call | solution.py:190
  118.5 5.4 %all-to-all-start = ((bf16[16,256,128]{2,1,0:T(8,128)(2,1)}), bf16[16,256,128]{2,1,0:T(8,128)(2,1)S(1)}, u32[]{:S(2)}, u32[]{:S(2)}) async-start(bf16[16,256,128]{2,1,0:T(8,128)(2,1)} %bitcast.20), calls=%async_computation | async-start | bytes 2097152 | tf_op jit(solution)/shard_map/all_to_all | solution.py:348
  124.3 16.8 %all-to-all-done.att_ref = bf16[16,256,128]{2,1,0:T(8,128)(2,1)S(1)} async-done(((bf16[16,256,128]{2,1,0:T(8,128)(2,1)}), bf16[16,256,128]{2,1,0:T(8,128)(2,1)S(1)}, u32[]{:S(2)}, u32[]{:S(2)}) %all-to-all-start) | async-done | bytes 1048608 | tf_op jit(solution)/shard_map/all_to_all | solution.py:348
  142.9 3.4 %all-to-all-start.1 = ((bf16[8,128,128]{2,1,0:T(8,128)(2,1)}), bf16[8,128,128]{2,1,0:T(8,128)(2,1)S(1)}, u32[]{:S(2)}, u32[]{:S(2)}) async-start(bf16[8,128,128]{2,1,0:T(8,128)(2,1)} %broadcast_in_dim.4), calls=%async_computation.1 | async-start | bytes 524288 | tf_op jit(solution)/shard_map/all_to_all | solution.py:357
  152.6 4.5 %collective-permute-start.17 = (bf16[64,128]{1,0:T(8,128)(2,1)S(1)}, bf16[64,128]{1,0:T(8,128)(2,1)S(1)}, u32[]{:S(2)}, u32[]{:S(2)}) collective-permute-start(bf16[64,128]{1,0:T(8,128)(2,1)S(1)} %get-tuple-element.59), channel_id=1, source_target_pairs={{0,4},{4,8},{8,12},{12,16},{16,20},{20,24},{24,28},{28,32},{32,36}... | collective-permute-start | bytes 49160 | tf_op jit(solution)/shard_map/ppermute | solution.py:368
  157.1 1.9 %collective-permute-start.18 = (bf16[64,128]{1,0:T(8,128)(2,1)S(1)}, bf16[64,128]{1,0:T(8,128)(2,1)S(1)}, u32[]{:S(2)}, u32[]{:S(2)}) collective-permute-start(bf16[64,128]{1,0:T(8,128)(2,1)S(1)} %get-tuple-element.58), channel_id=1, source_target_pairs={{4,0},{8,4},{12,8},{16,12},{20,16},{24,20},{28,24},{32,28},{36,32}... | collective-permute-start | bytes 49160 | tf_op jit(solution)/shard_map/ppermute | solution.py:369
  159.1 4.6 %collective-permute-done.18.after_ref = bf16[64,128]{1,0:T(8,128)(2,1)S(1)} collective-permute-done((bf16[64,128]{1,0:T(8,128)(2,1)S(1)}, bf16[64,128]{1,0:T(8,128)(2,1)S(1)}, u32[]{:S(2)}, u32[]{:S(2)}) %collective-permute-start.18) | collective-permute-done | bytes 16416 | tf_op jit(solution)/shard_map/ppermute | solution.py:369
  163.7 2.6 %shard_map.111 = bf16[512,8,128]{2,1,0:T(8,128)(2,1)} custom-call(s32[1]{0:T(128)} %dynamic_slice.20.limit_ref, bf16[128,128]{1,0:T(8,128)(2,1)S(1)} %dynamic-slice_bitcast_fusion.rows_ref, bf16[64,128]{1,0:T(8,128)(2,1)S(1)} %collective-permute-done.17.before_ref, bf16[64,128]{1,0:T(8,128)(2,1)S(1)} %collective-permute-done.18.after_ref, ...), custom_call_target="tpu_custom_call" | custom-call | tf_op jit(solution)/shard_map/pallas_call | solution.py:283
  (96 shorter events, 28.5 us)
Async XLA Ops:
  3.9 22.7 %collective-permute-start.3 = (bf16[256,3072]{1,0:T(8,128)(2,1)S(1)}, bf16[256,3072]{1,0:T(8,128)(2,1)}, u32[]{:S(2)}, u32[]{:S(2)}) collective-permute-start(bf16[256,3072]{1,0:T(8,128)(2,1)S(1)} %fusion.3.refs_0_), channel_id=1, source_target_pairs={{0,4},{4,0},{64,68},{68,64},{8,12},{12,8},{72,76},{76,72},{1,5},{5... | collective-permute-start | bytes 4718600 | tf_op jit(solution)/shard_map/ppermute | solution.py:32
  5.4 37.2 %collective-permute-start = (bf16[256,3072]{1,0:T(8,128)(2,1)S(1)}, bf16[256,3072]{1,0:T(8,128)(2,1)S(1)}, u32[]{:S(2)}, u32[]{:S(2)}) collective-permute-start(bf16[256,3072]{1,0:T(8,128)(2,1)S(1)} %fusion.3.refs_0_), channel_id=1, source_target_pairs={{0,16},{4,20},{64,80},{68,84},{8,24},{12,28},{72,88},{76,92},{1,17... | collective-permute-start | bytes 4718600 | tf_op jit(solution)/shard_map/ppermute | solution.py:32
  6.7 35.9 %collective-permute-start.1 = (bf16[256,3072]{1,0:T(8,128)(2,1)S(1)}, bf16[256,3072]{1,0:T(8,128)(2,1)}, u32[]{:S(2)}, u32[]{:S(2)}) collective-permute-start(bf16[256,3072]{1,0:T(8,128)(2,1)S(1)} %fusion.3.refs_0_), channel_id=1, source_target_pairs={{0,48},{4,52},{64,112},{68,116},{8,56},{12,60},{72,120},{76,124},{... | collective-permute-start | bytes 4718600 | tf_op jit(solution)/shard_map/ppermute | solution.py:32
  8.1 44.6 %copy-start = (bf16[3,3072,128]{2,1,0:T(8,128)(2,1)S(1)}, bf16[3,3072,128]{2,1,0:T(8,128)(2,1)}, u32[]{:S(2)}) copy-start(bf16[3,3072,128]{2,1,0:T(8,128)(2,1)} %refs_4_.1) | copy-start | bytes 7077892
  9.6 17.0 %collective-permute-start.2 = (bf16[3,768,128]{2,1,0:T(8,128)(2,1)S(1)}, bf16[3,768,128]{2,1,0:T(8,128)(2,1)S(1)}, u32[]{:S(2)}, u32[]{:S(2)}) collective-permute-start(bf16[3,768,128]{2,1,0:T(8,128)(2,1)S(1)} %get-tuple-element.57), channel_id=1, source_target_pairs={{0,72},{4,76},{64,8},{68,12},{8,64},{12,68},{72,0},{76,4},{1,73},{... | collective-permute-start | bytes 1769480 | tf_op jit(solution)/shard_map/ppermute | solution.py:32
  26.6 37.2 %copy-start.11 = (bf16[3,768,128]{2,1,0:T(8,128)(2,1)}, bf16[3,768,128]{2,1,0:T(8,128)(2,1)S(1)}, u32[]{:S(2)}) copy-start(bf16[3,768,128]{2,1,0:T(8,128)(2,1)S(1)} %collective-permute-done.2.refs_3_.refs_5_) | copy-start | bytes 1769476
  26.6 16.0 %collective-permute-start.4 = (bf16[3,768,128]{2,1,0:T(8,128)(2,1)S(1)}, bf16[3,768,128]{2,1,0:T(8,128)(2,1)S(1)}, u32[]{:S(2)}, u32[]{:S(2)}) collective-permute-start(bf16[3,768,128]{2,1,0:T(8,128)(2,1)S(1)} %collective-permute-done.2.refs_3_.refs_5_), channel_id=1, source_target_pairs={{0,3},{4,7},{64,67},{68,71},{8,11},{12,15},{72,75},{76,79},{1,0},{... | collective-permute-start | bytes 1769480 | tf_op jit(solution)/shard_map/ppermute | solution.py:32
  29.4 14.6 %collective-permute-start.5 = (bf16[3,768,128]{2,1,0:T(8,128)(2,1)S(1)}, bf16[3,768,128]{2,1,0:T(8,128)(2,1)S(1)}, u32[]{:S(2)}, u32[]{:S(2)}) collective-permute-start(bf16[3,768,128]{2,1,0:T(8,128)(2,1)S(1)} %get-tuple-element.29), channel_id=1, source_target_pairs={{0,72},{4,76},{64,8},{68,12},{8,64},{12,68},{72,0},{76,4},{1,73},{... | collective-permute-start | bytes 1769480 | tf_op jit(solution)/shard_map/ppermute | solution.py:32
  31.7 14.0 %collective-permute-start.6 = (bf16[3,768,128]{2,1,0:T(8,128)(2,1)S(1)}, bf16[3,768,128]{2,1,0:T(8,128)(2,1)S(1)}, u32[]{:S(2)}, u32[]{:S(2)}) collective-permute-start(bf16[3,768,128]{2,1,0:T(8,128)(2,1)S(1)} %collective-permute-done.2.refs_3_.refs_5_), channel_id=1, source_target_pairs={{0,1},{4,5},{64,65},{68,69},{8,9},{12,13},{72,73},{76,77},{1,2},{5... | collective-permute-start | bytes 1769480 | tf_op jit(solution)/shard_map/ppermute | solution.py:32
  45.7 11.2 %collective-permute-start.10 = (bf16[256,3072]{1,0:T(8,128)(2,1)S(1)}, bf16[256,3072]{1,0:T(8,128)(2,1)S(1)}, u32[]{:S(2)}, u32[]{:S(2)}) collective-permute-start(bf16[256,3072]{1,0:T(8,128)(2,1)S(1)} %collective-permute-done.refs_0_), channel_id=1, source_target_pairs={{0,4},{4,0},{64,68},{68,64},{8,12},{12,8},{72,76},{76,72},{1,5},{5... | collective-permute-start | bytes 4718600 | tf_op jit(solution)/shard_map/ppermute | solution.py:32
  48.7 15.1 %collective-permute-start.12 = (bf16[256,3072]{1,0:T(8,128)(2,1)}, bf16[256,3072]{1,0:T(8,128)(2,1)S(1)}, u32[]{:S(2)}, u32[]{:S(2)}) collective-permute-start(bf16[256,3072]{1,0:T(8,128)(2,1)} %collective-permute-done.1.refs_0_), channel_id=1, source_target_pairs={{0,4},{4,0},{64,68},{68,64},{8,12},{12,8},{72,76},{76,72},{1,5},{5... | collective-permute-start | bytes 4718600 | tf_op jit(solution)/shard_map/ppermute | solution.py:32
  49.9 20.2 %collective-permute-start.7 = (bf16[128,3072]{1,0:T(8,128)(2,1)S(1)}, bf16[128,3072]{1,0:T(8,128)(2,1)}, u32[]{:S(2)}, u32[]{:S(2)}) collective-permute-start(bf16[128,3072]{1,0:T(8,128)(2,1)S(1)} %slice.28), channel_id=1, source_target_pairs={{0,16},{4,20},{64,80},{68,84},{8,24},{12,28},{72,88},{76,92},{1,17... | collective-permute-start | bytes 2359304 | tf_op jit(solution)/shard_map/ppermute | solution.py:32
  50.0 20.1 %collective-permute-start.8 = (bf16[128,3072]{1,0:T(8,128)(2,1)S(1)}, bf16[128,3072]{1,0:T(8,128)(2,1)}, u32[]{:S(2)}, u32[]{:S(2)}) collective-permute-start(bf16[128,3072]{1,0:T(8,128)(2,1)S(1)} %slice.29), channel_id=1, source_target_pairs={{0,48},{4,52},{64,112},{68,116},{8,56},{12,60},{72,120},{76,124},{... | collective-permute-start | bytes 2359304 | tf_op jit(solution)/shard_map/ppermute | solution.py:32
  56.8 12.6 %collective-permute-start.9 = (bf16[3,512,128]{2,1,0:T(8,128)(2,1)S(1)}, bf16[3,512,128]{2,1,0:T(8,128)(2,1)S(1)}, u32[]{:S(2)}, u32[]{:S(2)}) collective-permute-start(bf16[3,512,128]{2,1,0:T(8,128)(2,1)S(1)} %get-tuple-element.37), channel_id=1, source_target_pairs={{0,8},{4,12},{64,72},{68,76},{8,0},{12,4},{72,64},{76,68},{1,9},{5... | collective-permute-start | bytes 1179656 | tf_op jit(solution)/shard_map/ppermute | solution.py:32
  60.8 15.5 %collective-permute-start.11 = (bf16[3,512,128]{2,1,0:T(8,128)(2,1)S(1)}, bf16[3,512,128]{2,1,0:T(8,128)(2,1)S(1)}, u32[]{:S(2)}, u32[]{:S(2)}) collective-permute-start(bf16[3,512,128]{2,1,0:T(8,128)(2,1)S(1)} %get-tuple-element.39), channel_id=1, source_target_pairs={{0,8},{4,12},{64,72},{68,76},{8,0},{12,4},{72,64},{76,68},{1,9},{5... | collective-permute-start | bytes 1179656 | tf_op jit(solution)/shard_map/ppermute | solution.py:32
  77.0 4.2 %collective-permute-start.13 = (bf16[128,3072]{1,0:T(8,128)(2,1)}, bf16[128,3072]{1,0:T(8,128)(2,1)}, u32[]{:S(2)}, u32[]{:S(2)}) collective-permute-start(bf16[128,3072]{1,0:T(8,128)(2,1)} %collective-permute-done.7.refs_0_), channel_id=1, source_target_pairs={{0,4},{4,0},{64,68},{68,64},{8,12},{12,8},{72,76},{76,72},{1,5},{5... | collective-permute-start | bytes 2359304 | tf_op jit(solution)/shard_map/ppermute | solution.py:32
  79.0 3.4 %collective-permute-start.14 = (bf16[128,3072]{1,0:T(8,128)(2,1)}, bf16[128,3072]{1,0:T(8,128)(2,1)}, u32[]{:S(2)}, u32[]{:S(2)}) collective-permute-start(bf16[128,3072]{1,0:T(8,128)(2,1)} %collective-permute-done.8.refs_1_), channel_id=1, source_target_pairs={{0,4},{4,0},{64,68},{68,64},{8,12},{12,8},{72,76},{76,72},{1,5},{5... | collective-permute-start | bytes 2359304 | tf_op jit(solution)/shard_map/ppermute | solution.py:32
  79.0 12.4 %collective-permute-start.15 = (bf16[3,512,128]{2,1,0:T(8,128)(2,1)}, bf16[3,512,128]{2,1,0:T(8,128)(2,1)}, u32[]{:S(2)}, u32[]{:S(2)}) collective-permute-start(bf16[3,512,128]{2,1,0:T(8,128)(2,1)} %get-tuple-element.49), channel_id=1, source_target_pairs={{0,8},{4,12},{64,72},{68,76},{8,0},{12,4},{72,64},{76,68},{1,9},{5... | collective-permute-start | bytes 1179656 | tf_op jit(solution)/shard_map/ppermute | solution.py:32
  91.2 16.3 %collective-permute-start.16 = (bf16[3,512,128]{2,1,0:T(8,128)(2,1)S(1)}, bf16[3,512,128]{2,1,0:T(8,128)(2,1)S(1)}, u32[]{:S(2)}, u32[]{:S(2)}) collective-permute-start(bf16[3,512,128]{2,1,0:T(8,128)(2,1)S(1)} %get-tuple-element.50), channel_id=1, source_target_pairs={{0,8},{4,12},{64,72},{68,76},{8,0},{12,4},{72,64},{76,68},{1,9},{5... | collective-permute-start | bytes 1179656 | tf_op jit(solution)/shard_map/ppermute | solution.py:32
  118.5 30.6 %copy-start.24 = (s32[8]{0:T(128)S(1)}, s32[8]{0:T(128)}, u32[]{:S(2)}) copy-start(s32[8]{0:T(128)} %param.15) | copy-start | bytes 100
  118.5 22.6 %all-to-all-start = ((bf16[16,256,128]{2,1,0:T(8,128)(2,1)}), bf16[16,256,128]{2,1,0:T(8,128)(2,1)S(1)}, u32[]{:S(2)}, u32[]{:S(2)}) async-start(bf16[16,256,128]{2,1,0:T(8,128)(2,1)} %bitcast.20), calls=%async_computation | async-start | bytes 2097152 | tf_op jit(solution)/shard_map/all_to_all | solution.py:348
  142.9 9.6 %all-to-all-start.1 = ((bf16[8,128,128]{2,1,0:T(8,128)(2,1)}), bf16[8,128,128]{2,1,0:T(8,128)(2,1)S(1)}, u32[]{:S(2)}, u32[]{:S(2)}) async-start(bf16[8,128,128]{2,1,0:T(8,128)(2,1)} %broadcast_in_dim.4), calls=%async_computation.1 | async-start | bytes 524288 | tf_op jit(solution)/shard_map/all_to_all | solution.py:357
  152.6 6.5 %collective-permute-start.17 = (bf16[64,128]{1,0:T(8,128)(2,1)S(1)}, bf16[64,128]{1,0:T(8,128)(2,1)S(1)}, u32[]{:S(2)}, u32[]{:S(2)}) collective-permute-start(bf16[64,128]{1,0:T(8,128)(2,1)S(1)} %get-tuple-element.59), channel_id=1, source_target_pairs={{0,4},{4,8},{8,12},{12,16},{16,20},{20,24},{24,28},{28,32},{32,36}... | collective-permute-start | bytes 49160 | tf_op jit(solution)/shard_map/ppermute | solution.py:368
  157.1 6.6 %collective-permute-start.18 = (bf16[64,128]{1,0:T(8,128)(2,1)S(1)}, bf16[64,128]{1,0:T(8,128)(2,1)S(1)}, u32[]{:S(2)}, u32[]{:S(2)}) collective-permute-start(bf16[64,128]{1,0:T(8,128)(2,1)S(1)} %get-tuple-element.58), channel_id=1, source_target_pairs={{4,0},{8,4},{12,8},{16,12},{20,16},{24,20},{28,24},{32,28},{36,32}... | collective-permute-start | bytes 49160 | tf_op jit(solution)/shard_map/ppermute | solution.py:369
  (22 other events, 247.6 us)
